TPU v7x, 128 devices: a whole 4x4x4 slice. The times are simulated.
128 devices in a mesh: grp: 8 (over z_hi, x), resp: 16 (over z_lo, y, core).
Axes of the slice: x: 4, y: 4, z: 4 (z_hi: 2, z_lo: 2; z = z_hi * 2 + z_lo), core: 2. Of those that a mesh axis runs over, the one named last changes fastest.
Arguments:
- queries: bfloat16 [8, 16, 256, 2560], P('grp', 'resp'), may hold values from -5 to 5
- resp_keys: bfloat16 [8, 16, 256, 512], P('grp', 'resp'), may hold values from -5 to 5
- resp_values: bfloat16 [8, 16, 256, 512], P('grp', 'resp'), may hold values from -5 to 5
- prompt_keys: bfloat16 [8, 2048, 512], P('grp', 'resp'), may hold values from -5 to 5
- prompt_values: bfloat16 [8, 2048, 512], P('grp', 'resp'), may hold values from -5 to 5
- out_grad: bfloat16 [8, 16, 256, 2560], P('grp', 'resp'), may hold values from -2.390625 to 2.390625
- lengths: int32 [8, 16], P('grp', 'resp'), may hold values from 32 to 256, as said below
- rewards: int32 [8, 16], P('grp', 'resp'), may hold values from 0 to 12, as said below
Outputs:
- attended: bfloat16 [8, 16, 256, 2560], P('grp', 'resp')
- grad_queries: bfloat16 [8, 16, 256, 2560], P('grp', 'resp')
- grad_resp_keys: bfloat16 [8, 16, 256, 512], P('grp', 'resp')
- grad_resp_values: bfloat16 [8, 16, 256, 512], P('grp', 'resp')
- grad_prompt_keys: bfloat16 [8, 2048, 512], P('grp', 'resp')
- grad_prompt_values: bfloat16 [8, 2048, 512], P('grp', 'resp')
Inputs may be any that keep to these rules, and one draw needn't show every extreme that they name: `lengths`: some response in every draw has the full length 256. Each group's rewards run from 0 up to a top score of that group, which some response reaches; one group's top is 12 and another's is 1.
All inputs are finite; a program needn't handle non-finite values.
Results may differ from a plain program's by a relative error of at most 0.03.
Values may be sent and summed in bfloat16 or wider, within the bound.
A program may use at most 128 MiB of HBM per device.

v0:
```python
import math

import jax
import jax.numpy as jnp
from jax import lax
from jax.sharding import PartitionSpec as P

DH = 128


def block_scan(block_step, state_now, keys_whole, values_whole):
    row_total = keys_whole.shape[0]
    block_rows = math.gcd(row_total, 512)
    key_blocks = keys_whole.reshape(row_total // block_rows, block_rows, keys_whole.shape[1])
    value_blocks = values_whole.reshape(row_total // block_rows, block_rows, values_whole.shape[1])

    def advance(state_in, blocks_in):
        return (block_step(state_in, blocks_in[0], blocks_in[1]), None)

    return lax.scan(advance, state_now, (key_blocks, value_blocks))[0]


def on_device(
    queries, resp_keys, resp_values, prompt_keys, prompt_values, out_grad, lengths, rewards
):
    inv_root = DH ** (-0.5)
    query_rows = queries[0, 0]
    row_total = query_rows.shape[0]
    groups = resp_keys.shape[-1] // DH
    head_count = query_rows.shape[-1] // DH
    query_heads = query_rows.reshape(row_total, groups, head_count // groups, DH)

    def logits_for(keys_piece):
        key_heads = keys_piece.reshape(keys_piece.shape[0], groups, DH)
        return (
            jnp.einsum("tghd,ngd->ghtn", query_heads, key_heads, preferred_element_type=jnp.float32)
            * inv_root
        )

    def weighted(soft_low, values_piece):
        value_heads = values_piece.reshape(values_piece.shape[0], groups, DH)
        return jnp.einsum(
            "ghtn,ngd->ghtd", soft_low, value_heads, preferred_element_type=jnp.float32
        )

    own_keys = resp_keys[0, 0]
    own_values = resp_values[0, 0]
    position = jnp.arange(row_total)
    causal = position[:, None] >= position[None, :]
    self_logits = jnp.where(causal, logits_for(own_keys), -jnp.inf)
    self_max = jnp.max(self_logits, axis=-1)
    start_state = (self_max, jnp.sum(jnp.exp(self_logits - self_max[..., None]), axis=-1))

    def total_step(state_in, keys_piece, values_piece):
        running_max, running_sum = state_in
        block_logits = logits_for(keys_piece)
        new_max = jnp.maximum(running_max, jnp.max(block_logits, axis=-1))
        factor = jnp.exp(running_max - new_max)
        return (
            new_max,
            running_sum * factor + jnp.sum(jnp.exp(block_logits - new_max[..., None]), axis=-1),
        )

    piece = lax.all_gather(prompt_keys, "resp", axis=1, tiled=True)
    final_state = block_scan(total_step, start_state, piece[0], piece[0])
    keys_whole, values_whole = (
        lax.all_gather(prompt_keys, "resp", axis=1, tiled=True),
        lax.all_gather(prompt_values, "resp", axis=1, tiled=True),
    )
    keys_all = keys_whole[0]
    values_all = values_whole[0]
    running_max, running_sum = final_state
    log_total = running_max + jnp.log(running_sum)

    def output_step(state_in, keys_piece, values_piece):
        block_soft = jnp.exp(logits_for(keys_piece) - log_total[..., None])
        return state_in + weighted(block_soft.astype(jnp.bfloat16), values_piece)

    self_out = weighted(
        jnp.exp(self_logits - log_total[..., None]).astype(jnp.bfloat16), own_values
    )
    accumulated = block_scan(output_step, self_out, keys_all, values_all)
    output_heads = accumulated.transpose(2, 0, 1, 3)
    attended = output_heads.reshape(row_total, head_count * DH).astype(jnp.bfloat16)
    reward_own = rewards[0, 0]
    length_own = lengths[0, 0]
    sum_one, sum_two = lax.psum((reward_own, reward_own * reward_own), "resp")
    live_total = lax.psum(length_own, ("grp", "resp"))
    resp_count = lax.axis_size("resp")
    sum_one = sum_one.astype(jnp.float32)
    sum_two = sum_two.astype(jnp.float32)
    mean_reward = sum_one / resp_count
    variance = (resp_count * sum_two - sum_one * sum_one) / (resp_count * resp_count)
    advantage = (reward_own.astype(jnp.float32) - mean_reward) / jnp.maximum(
        jnp.sqrt(variance), 1.0
    )
    norm_factor = lax.axis_size("grp") * resp_count * row_total / live_total.astype(jnp.float32)
    live_rows = (position < length_own).astype(jnp.float32)
    weights = advantage * norm_factor * live_rows
    grad_low = (out_grad[0, 0].astype(jnp.float32) * weights[:, None]).astype(jnp.bfloat16)
    grad_heads = grad_low.reshape(row_total, groups, head_count // groups, DH)
    attended_heads = attended.reshape(row_total, groups, head_count // groups, DH)
    row_delta = jnp.sum(
        grad_heads.astype(jnp.float32) * attended_heads.astype(jnp.float32), axis=-1
    ).transpose(1, 2, 0)

    def grad_terms(block_logits, keys_piece, values_piece):
        piece_rows = keys_piece.shape[0]
        key_heads = keys_piece.reshape(piece_rows, groups, DH)
        value_heads = values_piece.reshape(piece_rows, groups, DH)
        block_soft = jnp.exp(block_logits - log_total[..., None])
        grad_soft = jnp.einsum(
            "tghd,ngd->ghtn", grad_heads, value_heads, preferred_element_type=jnp.float32
        )
        grad_logits = (block_soft * (grad_soft - row_delta[..., None])).astype(jnp.bfloat16)
        soft_low = block_soft.astype(jnp.bfloat16)
        query_part = jnp.einsum(
            "ghtn,ngd->tghd", grad_logits, key_heads, preferred_element_type=jnp.float32
        )
        key_part = (
            jnp.einsum(
                "ghtn,tghd->ngd", grad_logits, query_heads, preferred_element_type=jnp.float32
            ).reshape(piece_rows, -1)
            * inv_root
        )
        value_part = jnp.einsum(
            "ghtn,tghd->ngd", soft_low, grad_heads, preferred_element_type=jnp.float32
        ).reshape(piece_rows, -1)
        return (query_part, key_part, value_part)

    self_terms = grad_terms(self_logits, own_keys, own_values)
    zero_query = jnp.zeros(query_heads.shape, jnp.float32)
    key_width = prompt_keys.shape[-1]
    prompt_total = keys_all.shape[0]
    block_rows = math.gcd(prompt_total, 512)
    key_blocks = keys_all.reshape(prompt_total // block_rows, block_rows, key_width)
    value_blocks = values_all.reshape(prompt_total // block_rows, block_rows, key_width)

    def full_step(state_in, blocks_in):
        terms_here = grad_terms(logits_for(blocks_in[0]), blocks_in[0], blocks_in[1])
        return (state_in + terms_here[0], (terms_here[1], terms_here[2]))

    query_sum, stacked_terms = lax.scan(full_step, zero_query, (key_blocks, value_blocks))
    prompt_key_grad, prompt_value_grad = (
        lax.psum_scatter(
            stacked_terms[0].reshape(prompt_total, key_width).astype(jnp.bfloat16),
            "resp",
            scatter_dimension=0,
            tiled=True,
        ).astype(jnp.float32),
        lax.psum_scatter(
            stacked_terms[1].reshape(prompt_total, key_width).astype(jnp.bfloat16),
            "resp",
            scatter_dimension=0,
            tiled=True,
        ).astype(jnp.float32),
    )
    grad_query = (
        ((self_terms[0] + query_sum) * inv_root)
        .reshape(row_total, head_count * DH)
        .astype(jnp.bfloat16)
    )
    return (
        attended[None, None],
        grad_query[None, None],
        self_terms[1].astype(jnp.bfloat16)[None, None],
        self_terms[2].astype(jnp.bfloat16)[None, None],
        prompt_key_grad.astype(jnp.bfloat16)[None],
        prompt_value_grad.astype(jnp.bfloat16)[None],
    )


def solution(mesh):
    return jax.shard_map(
        on_device,
        mesh=mesh,
        in_specs=(
            P("grp", "resp", None, None),
            P("grp", "resp", None, None),
            P("grp", "resp", None, None),
            P("grp", "resp", None),
            P("grp", "resp", None),
            P("grp", "resp", None, None),
            P("grp", "resp"),
            P("grp", "resp"),
        ),
        out_specs=(
            P("grp", "resp", None, None),
            P("grp", "resp", None, None),
            P("grp", "resp", None, None),
            P("grp", "resp", None, None),
            P("grp", "resp", None),
            P("grp", "resp", None),
        ),
        check_vma=False,
    )
```

profile of v0, /device:TPU:1, one launch (start us, length us, event | category | flops | bytes accessed | tf_op | source)
XLA Modules:
  0.0 367.3 jit_solution(13375908543098915984)
XLA Ops:
  8.7 68.7 %psum.23 = s32[]{:T(128)} all-reduce(s32[]{:T(128)} %bitcast.17), channel_id=1, replica_groups=mesh['grp'=8,'resp'=16] {'grp','resp'}, use_global_device_ids=true, to_apply=%region_10.11 | all-reduce | flops 1 | bytes 8 | tf_op jit(solution)/shard_map/psum | solution.py:88
  78.1 9.0 %all-reduce = (s32[]{:T(128)}, s32[]{:T(128)}) all-reduce(s32[]{:T(128)} %bitcast.18, s32[]{:T(128)S(6)} %mul.106), channel_id=1, replica_groups=mesh['grp'=8,'resp'=16] {'resp'}, use_global_device_ids=true, to_apply=%region_8.9 | all-reduce | flops 2 | bytes 16 | tf_op jit(solution)/shard_map/psum | solution.py:87
  91.0 1.8 reshape_squeeze.23
  94.2 2.9 copy.132
  98.2 2.3 copy-done.8
  100.5 1.1 exponential_reduce_fusion
  101.6 2.8 copy.124
  104.4 4.2 %copy.130 = bf16[4,512,512]{1,2,0:T(8,128)(2,1)} copy(bf16[4,512,512]{2,1,0:T(8,128)(2,1)} %bitcast.244) | data formatting | bytes 4194304 | tf_op jit(solution)/shard_map/while | solution.py:20
  108.6 13.8 %while.37 = (s32[]{:T(128)}, f32[4,5,256]{2,1,0:T(8,128)S(1)}, f32[4,5,256]{2,1,0:T(8,128)S(1)}, bf16[4,512,512]{1,2,0:T(8,128)(2,1)S(1)}, bf16[256,4,5,128]{3,0,2,1:T(8,128)(2,1)S(1)}, /*index=5*/s32[]{:T(128)}) while((s32[]{:T(128)}, f32[4,5,256]{2,1,0:T(8,128)S(1)}, f32[4,5,256]{2,1,0:T(8,128)S(1)}, bf16[4,512,512]{1,2,0:T(8,128)(2,1)S(1)}, ...), condition=%wide.region_5.6_spmd, body=%wide.region_2.5_spmd.sunk | while | flops 684206080 | bytes 24121424 | solution.py:20
  108.7 1.6 bitcast_reduce_fusion.2
  110.3 1.7 fusion.89
  112.1 1.6 bitcast_reduce_fusion.2
  113.7 1.7 fusion.89
  115.6 1.6 bitcast_reduce_fusion.2
  117.2 1.7 fusion.89
  119.1 1.6 bitcast_reduce_fusion.2
  120.7 1.7 fusion.89
  122.5 5.6 %fusion.34 = f32[4,5,256,128]{3,2,1,0:T(8,128)} fusion(bf16[256,4,128,1]{2,1,0,3:T(4,128)(2,1)} %bitcast.246, f32[4,256,256,5]{2,1,3,0:T(8,128)} %copy-done.8, f32[4,5,256]{2,1,0:T(8,128)S(1)} %log_add_fusion, pred[256,256]{0,1:T(8,128)(4,1)} %copy-done.13), kind=kOutput, calls=%fused_computation.54 | convolution fusion | flops 340787200 | bytes 8212480 | tf_op jit(solution)/shard_map/ghtn,ngd->ghtd/dot_general | solution.py:42
  128.1 38.2 %while.38 = (s32[]{:T(128)}, f32[4,5,256,128]{3,2,1,0:T(8,128)}, bf16[4,512,512]{1,2,0:T(8,128)(2,1)S(1)}, bf16[256,4,5,128]{3,0,2,1:T(8,128)(2,1)S(1)}, f32[4,5...) while((s32[]{:T(128)}, f32[4,5,256,128]{3,2,1,0:T(8,128)}, ...), condition=%wide.region_7.8_spmd, body=%wide.region_6.7_spmd.sunk | while | flops 1350696960 | bytes 9719897 | solution.py:20
  128.1 2.1 constant_dynamic-slice_fusion.10
  130.2 7.5 %fusion.94 = f32[4,5,256,128]{3,2,1,0:T(8,128)} fusion(f32[4,5,256,128]{3,2,1,0:T(8,128)} %get-tuple-element.468, bf16[512,4,128,1]{0,2,3,1:T(8,128)(2,1)} %bitcast.236, f32[4,5,256]{2,1,0:T(8,128)S(1)} %get-tuple-element.478, bf16[512,4,128,1]{0,2,3,1:T(8,128)(2,1)} %bitcast.237, bf16[256,4,5,128]{3,0,2,1:T(8,128)(2,1)S(1)} %get-tuple-element.477), kind=kOutput, calls=%fused_computation.13.clone.1 | convolution fusion | flops 1350696960 | bytes 7622656 | tf_op jit(solution)/shard_map/while/body/eval_jaxpr/ghtn,ngd->ghtd/dot_general | solution.py:42
  137.7 2.1 constant_dynamic-slice_fusion.10
  139.8 7.5 %fusion.94 = f32[4,5,256,128]{3,2,1,0:T(8,128)} fusion(f32[4,5,256,128]{3,2,1,0:T(8,128)} %get-tuple-element.468, bf16[512,4,128,1]{0,2,3,1:T(8,128)(2,1)} %bitcast.236, f32[4,5,256]{2,1,0:T(8,128)S(1)} %get-tuple-element.478, bf16[512,4,128,1]{0,2,3,1:T(8,128)(2,1)} %bitcast.237, bf16[256,4,5,128]{3,0,2,1:T(8,128)(2,1)S(1)} %get-tuple-element.477), kind=kOutput, calls=%fused_computation.13.clone.1 | convolution fusion | flops 1350696960 | bytes 7622656 | tf_op jit(solution)/shard_map/while/body/eval_jaxpr/ghtn,ngd->ghtd/dot_general | solution.py:42
  147.2 2.1 constant_dynamic-slice_fusion.10
  149.3 7.5 %fusion.94 = f32[4,5,256,128]{3,2,1,0:T(8,128)} fusion(f32[4,5,256,128]{3,2,1,0:T(8,128)} %get-tuple-element.468, bf16[512,4,128,1]{0,2,3,1:T(8,128)(2,1)} %bitcast.236, f32[4,5,256]{2,1,0:T(8,128)S(1)} %get-tuple-element.478, bf16[512,4,128,1]{0,2,3,1:T(8,128)(2,1)} %bitcast.237, bf16[256,4,5,128]{3,0,2,1:T(8,128)(2,1)S(1)} %get-tuple-element.477), kind=kOutput, calls=%fused_computation.13.clone.1 | convolution fusion | flops 1350696960 | bytes 7622656 | tf_op jit(solution)/shard_map/while/body/eval_jaxpr/ghtn,ngd->ghtd/dot_general | solution.py:42
  156.8 2.1 constant_dynamic-slice_fusion.10
  158.8 7.5 %fusion.94 = f32[4,5,256,128]{3,2,1,0:T(8,128)} fusion(f32[4,5,256,128]{3,2,1,0:T(8,128)} %get-tuple-element.468, bf16[512,4,128,1]{0,2,3,1:T(8,128)(2,1)} %bitcast.236, f32[4,5,256]{2,1,0:T(8,128)S(1)} %get-tuple-element.478, bf16[512,4,128,1]{0,2,3,1:T(8,128)(2,1)} %bitcast.237, bf16[256,4,5,128]{3,0,2,1:T(8,128)(2,1)S(1)} %get-tuple-element.477), kind=kOutput, calls=%fused_computation.13.clone.1 | convolution fusion | flops 1350696960 | bytes 7622656 | tf_op jit(solution)/shard_map/while/body/eval_jaxpr/ghtn,ngd->ghtd/dot_general | solution.py:42
  166.3 3.5 copy.131
  169.9 3.8 %multiply_reduce_fusion = (f32[256,4,5]{0,2,1:T(8,128)S(1)}, bf16[256,4,5,128]{0,3,2,1:T(8,128)(2,1)}) fusion(bf16[4,5,256,128]{2,3,1,0:T(8,128)(2,1)} %copy.131, f32[256,4,5,128]{0,3,2,1:T(8,128)} %bitcast.239, f32[256]{0:T(256)S(1)} %compare_select_fusion), kind=kLoop, calls=%fused_computation.45 | loop fusion | flops 3927040 | bytes 5264384 | tf_op jit(solution)/shard_map/reduce_sum | solution.py:103
  173.7 58.4 %while.39 = (s32[]{:T(128)}, f32[256,4,5,128]{0,3,2,1:T(8,128)S(1)}, bf16[4,512,512]{1,2,0:T(8,128)(2,1)}, bf16[4,512,512]{1,2,0:T(8,128)(2,1)}, bf16[4,512,512]...) while((s32[]{:T(128)}, ...), condition=%wide.region_13.14_spmd.clone, body=%wide.region_12.13_spmd.clone.sunk | while | flops 3378249728 | bytes 80277736 | solution.py:143
  173.7 1.2 constant_dynamic-slice_fusion.12
  176.0 1.6 fusion.105
  177.5 2.1 fusion.107
  179.6 4.4 %fusion.106 = bf16[4,5,256,512]{2,3,1,0:T(8,128)(2,1)S(1)} fusion(f32[4,512,256,5]{2,1,3,0:T(8,128)S(1)} %fusion.105, f32[4,5,256]{2,1,0:T(8,128)S(1)} %get-tuple-element.514, f32[4,5,256]{2,1,0:T(8,128)S(1)} %get-tuple-element.511, bf16[512,4,128,1]{0,2,3,1:T(8,128)(2,1)S(1)} %bitcast.233, bf16[256,4,5,128]{0,3,2,1:T(8,128)(2,1)} %get-tuple-element.513), kind=kOutput, calls=%fused_computation.19.clone.1 | convolution fusion | flops 684195840 | bytes 17604608 | tf_op jit(solution)/shard_map/while/body/eval_jaxpr/tghd,ngd->ghtn/dot_general | solution.py:112
  184.0 1.8 fusion.108
  185.9 1.3 bitcast_add_fusion.3
  188.2 1.2 constant_dynamic-slice_fusion.12
  190.5 1.6 fusion.105
  192.1 2.1 fusion.107
  194.2 4.4 %fusion.106 = bf16[4,5,256,512]{2,3,1,0:T(8,128)(2,1)S(1)} fusion(f32[4,512,256,5]{2,1,3,0:T(8,128)S(1)} %fusion.105, f32[4,5,256]{2,1,0:T(8,128)S(1)} %get-tuple-element.514, f32[4,5,256]{2,1,0:T(8,128)S(1)} %get-tuple-element.511, bf16[512,4,128,1]{0,2,3,1:T(8,128)(2,1)S(1)} %bitcast.233, bf16[256,4,5,128]{0,3,2,1:T(8,128)(2,1)} %get-tuple-element.513), kind=kOutput, calls=%fused_computation.19.clone.1 | convolution fusion | flops 684195840 | bytes 17604608 | tf_op jit(solution)/shard_map/while/body/eval_jaxpr/tghd,ngd->ghtn/dot_general | solution.py:112
  198.6 1.8 fusion.108
  200.4 1.3 bitcast_add_fusion.3
  202.8 1.2 constant_dynamic-slice_fusion.12
  205.1 1.6 fusion.105
  206.7 2.1 fusion.107
  208.8 4.4 %fusion.106 = bf16[4,5,256,512]{2,3,1,0:T(8,128)(2,1)S(1)} fusion(f32[4,512,256,5]{2,1,3,0:T(8,128)S(1)} %fusion.105, f32[4,5,256]{2,1,0:T(8,128)S(1)} %get-tuple-element.514, f32[4,5,256]{2,1,0:T(8,128)S(1)} %get-tuple-element.511, bf16[512,4,128,1]{0,2,3,1:T(8,128)(2,1)S(1)} %bitcast.233, bf16[256,4,5,128]{0,3,2,1:T(8,128)(2,1)} %get-tuple-element.513), kind=kOutput, calls=%fused_computation.19.clone.1 | convolution fusion | flops 684195840 | bytes 17604608 | tf_op jit(solution)/shard_map/while/body/eval_jaxpr/tghd,ngd->ghtn/dot_general | solution.py:112
  213.2 1.8 fusion.108
  215.0 1.3 bitcast_add_fusion.3
  217.4 1.2 constant_dynamic-slice_fusion.12
  219.7 1.6 fusion.105
  221.3 2.1 fusion.107
  223.4 4.4 %fusion.106 = bf16[4,5,256,512]{2,3,1,0:T(8,128)(2,1)S(1)} fusion(f32[4,512,256,5]{2,1,3,0:T(8,128)S(1)} %fusion.105, f32[4,5,256]{2,1,0:T(8,128)S(1)} %get-tuple-element.514, f32[4,5,256]{2,1,0:T(8,128)S(1)} %get-tuple-element.511, bf16[512,4,128,1]{0,2,3,1:T(8,128)(2,1)S(1)} %bitcast.233, bf16[256,4,5,128]{0,3,2,1:T(8,128)(2,1)} %get-tuple-element.513), kind=kOutput, calls=%fused_computation.19.clone.1 | convolution fusion | flops 684195840 | bytes 17604608 | tf_op jit(solution)/shard_map/while/body/eval_jaxpr/tghd,ngd->ghtn/dot_general | solution.py:112
  227.8 1.8 fusion.108
  229.6 1.3 bitcast_add_fusion.3
  231.0 1.1 bitcast_dynamic-update-slice_fusion.2
  232.1 4.2 %copy.143 = bf16[4,512,512]{2,1,0:T(8,128)(2,1)} copy(bf16[4,512,512]{1,2,0:T(8,128)(2,1)} %get-tuple-element.125) | data formatting | bytes 4194304 | tf_op jit(solution)/shard_map/convert_element_type | solution.py:152
  236.3 4.4 %copy.142 = bf16[4,512,512]{2,1,0:T(8,128)(2,1)} copy(bf16[4,512,512]{1,2,0:T(8,128)(2,1)} %get-tuple-element.124) | data formatting | bytes 4194304 | tf_op jit(solution)/shard_map/convert_element_type | solution.py:146
  240.7 2.5 copy.144
  243.2 4.6 %fusion.25 = bf16[4,5,256,256]{2,3,1,0:T(8,128)(2,1)S(1)} fusion(f32[4,256,256,5]{2,1,3,0:T(8,128)} %copy-done.8, f32[4,5,256]{2,1,0:T(8,128)S(1)} %get-tuple-element.535, f32[4,5,256]{2,1,0:T(8,128)S(1)} %get-tuple-element.534, pred[256,256]{0,1:T(8,128)(4,1)S(1)} %copy-done.14, bf16[256,4,5,128]{0,3,2,1:T(8,128)(2,1)} %get-tuple-element.525, ...), kind=kOutput, calls=%fused_computation.36 | convolution fusion | flops 343408640 | bytes 9543680 | tf_op jit(solution)/shard_map/tghd,ngd->ghtn/dot_general | solution.py:112
  250.2 3.4 fusion.29
  253.6 2.5 copy.145
  256.2 3.8 %fusion.32 = bf16[4,128,256]{2,1,0:T(8,128)(2,1)S(1)} fusion(bf16[256,4,5,128]{0,3,2,1:T(8,128)(2,1)S(1)} %copy-done.7, f32[4,256,256,5]{2,1,3,0:T(8,128)} %copy-done.8, f32[4,5,256]{2,1,0:T(8,128)S(1)} %get-tuple-element.534, pred[256,256]{0,1:T(8,128)(4,1)S(1)} %copy-done.14), kind=kOutput, calls=%fused_computation.51 | convolution fusion | flops 340918272 | bytes 6901760 | tf_op jit(solution)/shard_map/ghtn,tghd->ngd/dot_general | solution.py:126
  260.9 35.2 %reduce-scatter.5.cloned.1.call-done = bf16[128,512]{1,0:T(8,128)(2,1)} async-done(((bf16[2048,512]{1,0:T(8,128)(2,1)}), bf16[128,512]{1,0:T(8,128)(2,1)}) %reduce-scatter.5.cloned.1.call-update) | async-done | bytes 131088 | tf_op jit(solution)/shard_map/reduce_scatter | solution.py:151
  296.1 64.7 %reduce-scatter.3.cloned.1.call-done = bf16[128,512]{1,0:T(8,128)(2,1)} async-done(((bf16[2048,512]{1,0:T(8,128)(2,1)}), bf16[128,512]{1,0:T(8,128)(2,1)}) %reduce-scatter.3.cloned.1.call-update) | async-done | bytes 131088 | tf_op jit(solution)/shard_map/reduce_scatter | solution.py:145
  (96 shorter events, 16.2 us)
Async XLA Ops:
  7.2 85.6 %copy-start.12 = (bf16[1,1,256,2560]{3,2,1,0:T(8,128)(2,1)S(1)}, bf16[1,1,256,2560]{3,2,1,0:T(8,128)(2,1)}, u32[]{:S(2)}) copy-start(bf16[1,1,256,2560]{3,2,1,0:T(8,128)(2,1)} %param.14) | copy-start | bytes 3932164
  7.2 94.4 %all-gather.3.cloned.1.call-start = ((), (), s32[]{:S(2)}) async-start(), calls=%async_computation.2 | async-start | bytes 2228224 | tf_op jit(solution)/shard_map/all_gather | solution.py:64
  7.9 96.5 %all-gather.5.cloned.1.call-start = ((), (), s32[]{:S(2)}) async-start(), calls=%async_computation.3 | async-start | bytes 2228224 | tf_op jit(solution)/shard_map/all_gather | solution.py:68
  8.7 287.4 %reduce-scatter.5.cloned.1.call-start = ((), (), s32[]{:S(2)}) async-start(), calls=%async_computation.5 | async-start | bytes 2228224 | tf_op jit(solution)/shard_map/reduce_scatter | solution.py:151
  91.0 6.3 %copy-start.10 = (bf16[256,4,128,1]{0,2,3,1:T(8,128)(2,1)}, bf16[256,4,128,1]{0,2,3,1:T(8,128)(2,1)S(1)}, u32[]{:S(2)}) copy-start(bf16[256,4,128,1]{0,2,3,1:T(8,128)(2,1)S(1)} %copy.170) | copy-start | bytes 786436
  93.4 3.8 %copy-start.1 = (bf16[1,1,256,2560]{2,3,1,0:T(8,128)(2,1)}, bf16[1,1,256,2560]{2,3,1,0:T(8,128)(2,1)S(1)}, u32[]{:S(2)}) copy-start(bf16[1,1,256,2560]{2,3,1,0:T(8,128)(2,1)S(1)} %copy.121) | copy-start | bytes 3932164
  97.2 1.0 copy-start.13
  98.2 2.3 copy-start.8
  166.3 3.5 copy-start.5
  169.8 3.8 %copy-start = (f32[256,4,5,128]{0,3,2,1:T(8,128)S(1)}, f32[256,4,5,128]{0,3,2,1:T(8,128)}, u32[]{:S(2)}) copy-start(f32[256,4,5,128]{0,3,2,1:T(8,128)} %custom-call) | copy-start | bytes 7864324
  173.7 2.3 copy-start.2
  175.9 1.6 copy-start.6
  179.6 4.4 %copy-start.3 = (bf16[256,4,5,128]{0,3,2,1:T(8,128)(2,1)S(1)}, bf16[256,4,5,128]{0,3,2,1:T(8,128)(2,1)}, u32[]{:S(2)}) copy-start(bf16[256,4,5,128]{0,3,2,1:T(8,128)(2,1)} %get-tuple-element.510) | copy-start | bytes 3932164 | tf_op jit(solution)/shard_map/while
  188.2 2.3 copy-start.2
  190.5 1.6 copy-start.6
  194.2 4.4 %copy-start.3 = (bf16[256,4,5,128]{0,3,2,1:T(8,128)(2,1)S(1)}, bf16[256,4,5,128]{0,3,2,1:T(8,128)(2,1)}, u32[]{:S(2)}) copy-start(bf16[256,4,5,128]{0,3,2,1:T(8,128)(2,1)} %get-tuple-element.510) | copy-start | bytes 3932164 | tf_op jit(solution)/shard_map/while
  202.8 2.3 copy-start.2
  205.1 1.6 copy-start.6
  208.8 4.4 %copy-start.3 = (bf16[256,4,5,128]{0,3,2,1:T(8,128)(2,1)S(1)}, bf16[256,4,5,128]{0,3,2,1:T(8,128)(2,1)}, u32[]{:S(2)}) copy-start(bf16[256,4,5,128]{0,3,2,1:T(8,128)(2,1)} %get-tuple-element.510) | copy-start | bytes 3932164 | tf_op jit(solution)/shard_map/while
  217.4 2.3 copy-start.2
  219.7 1.6 copy-start.6
  223.4 4.4 %copy-start.3 = (bf16[256,4,5,128]{0,3,2,1:T(8,128)(2,1)S(1)}, bf16[256,4,5,128]{0,3,2,1:T(8,128)(2,1)}, u32[]{:S(2)}) copy-start(bf16[256,4,5,128]{0,3,2,1:T(8,128)(2,1)} %get-tuple-element.510) | copy-start | bytes 3932164 | tf_op jit(solution)/shard_map/while
  236.3 124.5 %reduce-scatter.3.cloned.1.call-start = ((), (), s32[]{:S(2)}) async-start(), calls=%async_computation.4 | async-start | bytes 2228224 | tf_op jit(solution)/shard_map/reduce_scatter | solution.py:145
  240.7 2.5 copy-start.14
  240.7 2.5 copy-start.15
  243.2 4.6 %copy-start.4 = (bf16[256,4,5,128]{0,3,2,1:T(8,128)(2,1)S(1)}, bf16[256,4,5,128]{0,3,2,1:T(8,128)(2,1)}, u32[]{:S(2)}) copy-start(bf16[256,4,5,128]{0,3,2,1:T(8,128)(2,1)} %get-tuple-element.522) | copy-start | bytes 3932164
  247.8 1.5 copy-start.9
  247.8 2.3 copy-start.11
  253.6 2.5 copy-start.7
Sparse Core Ops, SparseCore 0:
  9.7 37.4 all-gather.2
  48.9 34.2 all-gather.4
  236.4 59.6 reduce-scatter.4
  298.9 61.8 reduce-scatter.2
where the time goes:
time: 372 us; the launch traced here: 367 us
  waiting for transfers between devices  101 us (27%)
  matrix products  100 us (27%)
  blocking collectives  77.7 us (21%)
  local copies, waits for them, and re-layouts  57.7 us (16%)
  between operations  17.4 us (5%)
  other arithmetic  12 us (3%)
    psum x1, blocking collectives, on_device(): live_total = lax.psum(length_own, ('grp', 'resp'))  68.7 us
    reduce_scatter x1, waiting for transfers between devices, on_device(): lax.psum_scatter(stacked_terms[0].reshape(prompt_total, key_width).astype...  64.7 us
    dot_general x5, matrix products, weighted(): jnp.einsum('ghtn,ngd->ghtd', soft_low, value_heads, preferred_element_typ...  35.5 us
    reduce_scatter x1, waiting for transfers between devices, on_device(): lax.psum_scatter(stacked_terms[1].reshape(prompt_total, key_width).astype...  35.2 us
    dot_general x5, matrix products, grad_terms(): jnp.einsum('tghd,ngd->ghtn', grad_heads, value_heads, preferred_element_t...  22.3 us
    dynamic_slice x16, local copies, waits for them, and re-layouts, block_scan(): return lax.scan(advance, state_now, (key_blocks, value_blocks))[0]  17.5 us
    dot_general x9, matrix products, logits_for(): jnp.einsum('tghd,ngd->ghtn', query_heads, key_heads, preferred_element_ty...  13.6 us
    dot_general x5, matrix products, grad_terms(): jnp.einsum('ghtn,tghd->ngd', soft_low, grad_heads, preferred_element_type...  12.1 us
  transfers between devices with their start and end apart: 4, of which 2 were waited for; matrix products, arithmetic and copies ran while one was open for 10% of the time, Pallas kernels for 0%

commit v1 on v0

v1 whole, which is shorter than its diff:
```python
import math

import jax
import jax.numpy as jnp
from jax import lax
from jax.experimental import pallas as pl
from jax.experimental.pallas import tpu as pltpu
from jax.sharding import PartitionSpec as P

DH = 128
F32 = jnp.float32
BF16 = jnp.bfloat16
MESH = pl.DeviceIdType.MESH

SLOTS = ((0, 0), (0, 3), (0, 1), (1, 0), (1, 3), (0, 2), (1, 1), (1, 2))
OWN, YM, YP, ZZ, ZYM, YY, ZYP, ZYY = range(8)


def nn(a, b):
    return jnp.dot(a, b, preferred_element_type=F32)


def nt(a, b):
    return lax.dot_general(a, b, (((1,), (1,)), ((), ())), preferred_element_type=F32)


def kernel(
    n_grp, heads_per, q_hbm, rk_hbm, rv_hbm, pk_hbm, pv_hbm, og_hbm, len_ref, rew_ref,
    att_hbm, dq_hbm, drk_hbm, drv_hbm, dpk_hbm, dpv_hbm,
    qn, gn, rkn, rvn, kvn, qT, gT, e_st, m_st, m_cur, l_cur, acc, dqa, ds, aux,
    stat_out, stat_in, glen_out, glen_in, snd, rcv, own_part, att_n, dq_n, rg_n, pg_n,
    sem_l, sem_ps, sem_pr, sem_as, sem_ar, sem_ss, sem_sr, sem_gs, sem_gr,
    sem_ms, sem_mr, sem_ol, sem_os, sem_or,
):
    rows = qn.shape[1]
    half_q = qn.shape[2]
    half_k = rkn.shape[2]
    piece = pk_hbm.shape[1]
    blk = 2 * piece
    width = heads_per * rows
    inv_root = DH ** (-0.5)
    scale2 = inv_root * math.log2(math.e)
    me = lax.axis_index("resp")
    grp = lax.axis_index("grp")
    z = me // 8
    y = (me // 2) % 4
    c = me % 2

    def at(dz, dy, dc):
        return {"resp": ((z + dz) % 2) * 8 + ((y + dy) % 4) * 2 + (c + dc) % 2}

    def to(src, dst, s_sem, r_sem, target):
        return pltpu.make_async_remote_copy(
            src_ref=src, dst_ref=dst, send_sem=s_sem, recv_sem=r_sem,
            device_id=target, device_id_type=MESH,
        )

    cq = pl.ds(pl.multiple_of(c * half_q, half_q), half_q)
    oq = pl.ds(pl.multiple_of((1 - c) * half_q, half_q), half_q)
    ck = pl.ds(pl.multiple_of(c * half_k, half_k), half_k)
    ok = pl.ds(pl.multiple_of((1 - c) * half_k, half_k), half_k)
    my_rows = pl.ds(pl.multiple_of(c * piece, piece), piece)

    local = [
        pltpu.make_async_copy(pk_hbm.at[0, :, ck], kvn.at[OWN, 0, my_rows, :], sem_l.at[0]),
        pltpu.make_async_copy(pv_hbm.at[0, :, ck], kvn.at[OWN, 1, my_rows, :], sem_l.at[1]),
        pltpu.make_async_copy(q_hbm.at[0, 0, :, cq], qn.at[0], sem_l.at[2]),
        pltpu.make_async_copy(rk_hbm.at[0, 0, :, ck], rkn.at[0], sem_l.at[3]),
        pltpu.make_async_copy(rv_hbm.at[0, 0, :, ck], rvn.at[0], sem_l.at[4]),
        pltpu.make_async_copy(og_hbm.at[0, 0, :, cq], gn.at[0], sem_l.at[5]),
    ]
    for cp in local:
        cp.start()

    row_id = lax.broadcasted_iota(jnp.int32, (8, 128), 0)
    stat_out[...] = jnp.where(row_id == 0, len_ref[0, 0], rew_ref[0, 0])

    others = [
        (dz, dy, dc) for dz in range(2) for dy in range(4) for dc in range(2) if dz or dy or dc
    ]
    barrier = pltpu.get_barrier_semaphore()
    for dz, dy, dc in others:
        pl.semaphore_signal(barrier, inc=1, device_id=at(dz, dy, dc), device_id_type=MESH)
    for dg in range(1, n_grp):
        pl.semaphore_signal(
            barrier, inc=1, device_id={"grp": (grp + dg) % n_grp}, device_id_type=MESH
        )
    pl.semaphore_wait(barrier, len(others) + n_grp - 1)

    twin = at(0, 0, 1)
    pair = [
        to(pk_hbm.at[0, :, ok], kvn.at[OWN, 0, my_rows, :], sem_ps.at[0], sem_pr.at[0], twin),
        to(pv_hbm.at[0, :, ok], kvn.at[OWN, 1, my_rows, :], sem_ps.at[1], sem_pr.at[1], twin),
        to(q_hbm.at[0, 0, :, oq], qn.at[1], sem_ps.at[2], sem_pr.at[2], twin),
        to(rk_hbm.at[0, 0, :, ok], rkn.at[1], sem_ps.at[3], sem_pr.at[3], twin),
        to(rv_hbm.at[0, 0, :, ok], rvn.at[1], sem_ps.at[4], sem_pr.at[4], twin),
        to(og_hbm.at[0, 0, :, oq], gn.at[1], sem_ps.at[5], sem_pr.at[5], twin),
    ]
    for cp in pair:
        cp.start()

    z_to, up, down = at(1, 0, 0), at(0, 1, 0), at(0, 3, 0)
    ag_plan = (
        (OWN, ZZ, 0, z_to), (OWN, YM, 0, up), (OWN, YP, 0, down),
        (OWN, ZZ, 1, z_to), (OWN, YM, 1, up), (OWN, YP, 1, down),
        (YM, YY, 0, up), (YM, ZYM, 0, z_to), (YM, ZYM, 1, z_to),
        (YP, YY, 1, down), (ZZ, ZYP, 0, down), (ZZ, ZYP, 1, down),
        (ZYM, ZYY, 0, up), (ZYM, ZYY, 1, up),
    )
    ag = {}
    for src, dst, kv, target in ag_plan:
        ag[dst, kv] = to(
            kvn.at[src, kv], kvn.at[dst, kv], sem_as.at[dst, kv], sem_ar.at[dst, kv], target
        )

    for i in (0, 1):
        local[i].wait()
        pair[i].wait_recv()
    for kv in (0, 1):
        for dst in (ZZ, YM, YP):
            ag[dst, kv].start()

    stats = []
    for n, (dz, dy, dc) in enumerate(others):
        slot = ((-dz) % 2) * 8 + ((-dy) % 4) * 2 + dc
        stats.append(
            to(stat_out, stat_in.at[slot], sem_ss.at[slot], sem_sr.at[slot], at(dz, dy, dc))
        )
        stats[-1].start()

    def turn(src, dst, r):
        for j in range(2):
            for h in range(heads_per):
                dst[2 * r + j, :, h * rows:(h + 1) * rows] = src[
                    r, :, (j * heads_per + h) * DH:(j * heads_per + h + 1) * DH
                ].T

    def forward(k, vt, u, block, first):
        for h in range(heads_per):
            cols = slice(h * rows, (h + 1) * rows)
            s = nn(k, qT[u, :, cols])
            if first:
                seen = lax.broadcasted_iota(jnp.int32, s.shape, 0) <= (
                    lax.broadcasted_iota(jnp.int32, s.shape, 1)
                )
                s = jnp.where(seen, s, -jnp.inf)
                m_new = jnp.max(s, axis=0, keepdims=True)
            else:
                m_old = m_cur[u:u + 1, cols]
                m_new = jnp.maximum(m_old, jnp.max(s, axis=0, keepdims=True))
            e = jnp.exp2(s * scale2 - m_new * scale2)
            total = jnp.sum(e, axis=0, keepdims=True)
            low = e.astype(BF16)
            e_st[block, u, :, cols] = low
            part = nn(vt, low)
            if first:
                l_cur[u:u + 1, cols] = total
                acc[u, :, cols] = part
            else:
                alpha = jnp.exp2((m_old - m_new) * scale2)
                l_cur[u:u + 1, cols] = l_cur[u:u + 1, cols] * alpha + total
                acc[u, :, cols] = acc[u, :, cols] * alpha + part
            m_cur[u:u + 1, cols] = m_new
            m_st[block, u:u + 1, cols] = m_new

    n_blocks = 8
    for r in range(2):
        if r == 0:
            for i in (2, 3, 4):
                local[i].wait()
        else:
            for i in (2, 3, 4):
                pair[i].wait_recv()
        turn(qn, qT, r)
        for j in range(2):
            heads = slice(j * DH, (j + 1) * DH)
            forward(rkn[r, :, heads], rvn[r, :, heads].T, 2 * r + j, n_blocks, True)

    for cp in stats:
        cp.wait_recv()
    sum_one = stat_out[1:2, :]
    sum_two = sum_one * sum_one
    live = stat_out[0:1, :]
    for slot in range(1, 16):
        one = stat_in[slot, 1:2, :]
        sum_one = sum_one + one
        sum_two = sum_two + one * one
        live = live + stat_in[slot, 0:1, :]
    glen_out[...] = jnp.broadcast_to(live, (8, 128))
    glens = []
    for dg in range(1, n_grp):
        glens.append(
            to(
                glen_out, glen_in.at[n_grp - dg], sem_gs.at[n_grp - dg], sem_gr.at[n_grp - dg],
                {"grp": (grp + dg) % n_grp},
            )
        )
        glens[-1].start()

    def pass_on(waits, starts):
        for key in waits:
            ag[key].wait_recv()
        for key in starts:
            ag[key].start()

    @pl.loop(0, n_blocks)
    def forward_step(step):
        @pl.when(step == 1)
        def _():
            pass_on([(YM, 0)], [(YY, 0), (ZYM, 0)])
            pass_on([(ZZ, 0)], [(ZYP, 0)])
            pass_on([(YM, 1)], [(ZYM, 1)])
            pass_on([(YP, 0), (YP, 1)], [(YY, 1)])
            pass_on([(ZZ, 1)], [(ZYP, 1)])

        @pl.when(step == 4)
        def _():
            pass_on([(ZYM, 0)], [(ZYY, 0)])
            pass_on([(ZYM, 1)], [(ZYY, 1)])

        @pl.when(step == 5)
        def _():
            pass_on([(YY, 0), (YY, 1)], [])

        @pl.when(step == 6)
        def _():
            pass_on([(ZYP, 0), (ZYP, 1)], [])

        @pl.when(step == 7)
        def _():
            pass_on([(ZYY, 0), (ZYY, 1)], [])

        for j in range(2):
            heads = slice(j * DH, (j + 1) * DH)
            k = kvn[step, 0, :, heads]
            vt = kvn[step, 1, :, heads].T
            for r in range(2):
                forward(k, vt, 2 * r + j, step, False)

    for cp in glens:
        cp.wait_recv()
    for slot in range(1, n_grp):
        live = live + glen_in[slot, 0:1, :]
    n_resp = 16
    sum_one = sum_one.astype(F32)
    sum_two = sum_two.astype(F32)
    mean = sum_one / n_resp
    variance = (n_resp * sum_two - sum_one * sum_one) / (n_resp * n_resp)
    spread = jnp.maximum(jnp.sqrt(variance), 1.0)
    norm = (n_grp * n_resp * rows) / live.astype(F32)
    local[5].wait()
    pair[5].wait_recv()
    for r in range(2):
        turn(gn, gT, r)
        length = stat_out[0:1, :] if r == 0 else stat_in[1, 0:1, :]
        reward = stat_out[1:2, :] if r == 0 else stat_in[1, 1:2, :]
        strength = (reward.astype(F32) - mean) / spread * norm
        weight = jnp.concatenate(
            [
                jnp.where(
                    lax.broadcasted_iota(jnp.int32, (1, 128), 1) + start < length, strength, 0.0
                )
                for start in range(0, rows, 128)
            ],
            axis=1,
        )
        for j in range(2):
            u = 2 * r + j
            for h in range(heads_per):
                cols = slice(h * rows, (h + 1) * rows)
                inv = 1.0 / l_cur[u:u + 1, cols]
                out = (acc[u, :, cols] * inv).astype(BF16)
                col = slice((j * heads_per + h) * DH, (j * heads_per + h + 1) * DH)
                att_n[r, :, col] = out.T
                delta = jnp.sum(
                    out.astype(F32) * gT[u, :, cols].astype(F32), axis=0, keepdims=True
                )
                aux[0, u:u + 1, cols] = inv * weight
                aux[1, u:u + 1, cols] = delta
                dqa[u, :, cols] = jnp.zeros((DH, rows), F32)

    att_own = pltpu.make_async_copy(att_n.at[0], att_hbm.at[0, 0, :, cq], sem_ol.at[0])
    att_twin = to(att_n.at[1], att_hbm.at[0, 0, :, cq], sem_os.at[0], sem_or.at[0], twin)
    att_own.start()
    att_twin.start()

    def backward(k, v, kt, u, block, tmp):
        scaled = []
        for h in range(heads_per):
            cols = slice(h * rows, (h + 1) * rows)
            m_fin = m_cur[u:u + 1, cols]
            factor = jnp.exp2((m_st[block, u:u + 1, cols] - m_fin) * scale2) * aux[0, u:u + 1, cols]
            g = (gT[u, :, cols].astype(F32) * factor).astype(BF16)
            scaled.append(g)
            d = nn(v, g) - factor * aux[1, u:u + 1, cols]
            low = (e_st[block, u, :, cols].astype(F32) * d).astype(BF16)
            ds[tmp, :, cols] = low
            dqa[u, :, cols] = dqa[u, :, cols] + nn(kt, low)
        g_all = jnp.concatenate(scaled, axis=1)
        return nt(qT[u], ds[tmp]) * inv_root, nt(g_all, e_st[block, u])

    names = ("m1", "m6", "m3", "m2", "m7", "m5", "m4")
    route = {
        "m1": (down, down), "m6": (up, up), "m3": (down, up), "m2": (z_to, z_to),
        "m7": (z_to, z_to), "m5": (up, up), "m4": (down, down),
    }
    msg = {}
    for n, name in enumerate(names):
        for kv in range(2):
            msg[name, kv] = to(
                snd.at[n, kv], rcv.at[n, kv], sem_ms.at[n, kv], sem_mr.at[n, kv], route[name][kv]
            )

    needs = {
        0: ((), ()), 1: ((), ()), 2: ((), ()), 3: (("m1",), ("m1",)), 4: (("m6",), ("m6",)),
        5: ((), ("m3",)), 6: (("m2", "m3"), ("m2",)),
    }

    @pl.loop(0, n_blocks)
    def backward_step(step):
        block = n_blocks - 1 - step
        for j in range(2):
            heads = slice(j * DH, (j + 1) * DH)
            k = kvn[block, 0, :, heads]
            v = kvn[block, 1, :, heads]
            kt = k.T
            first = backward(k, v, kt, j, block, 2 * j)
            second = backward(k, v, kt, 2 + j, block, 2 * j + 1)
            own_part[0, heads, :] = first[0] + second[0]
            own_part[1, heads, :] = first[1] + second[1]

        for n, name in enumerate(names):
            @pl.when(step == n)
            def _():
                for kv in range(2):
                    total = own_part[kv]
                    for other in needs[n][kv]:
                        msg[other, kv].wait_recv()
                        total = total + rcv[names.index(other), kv].astype(F32)
                    snd[n, kv] = total.astype(BF16)
                    msg[name, kv].start()

    for r in range(2):
        for j in range(2):
            heads = slice(j * DH, (j + 1) * DH)
            k = rkn[r, :, heads]
            v = rvn[r, :, heads]
            grad_k, grad_v = backward(k, v, k.T, 2 * r + j, n_blocks, j)
            rg_n[r, 0, :, heads] = grad_k.astype(BF16).T
            rg_n[r, 1, :, heads] = grad_v.astype(BF16).T
    outs_own = [
        pltpu.make_async_copy(rg_n.at[0, 0], drk_hbm.at[0, 0, :, ck], sem_ol.at[1]),
        pltpu.make_async_copy(rg_n.at[0, 1], drv_hbm.at[0, 0, :, ck], sem_ol.at[2]),
        pltpu.make_async_copy(dq_n.at[0], dq_hbm.at[0, 0, :, cq], sem_ol.at[3]),
    ]
    outs_twin = [
        to(rg_n.at[1, 0], drk_hbm.at[0, 0, :, ck], sem_os.at[1], sem_or.at[1], twin),
        to(rg_n.at[1, 1], drv_hbm.at[0, 0, :, ck], sem_os.at[2], sem_or.at[2], twin),
        to(dq_n.at[1], dq_hbm.at[0, 0, :, cq], sem_os.at[3], sem_or.at[3], twin),
    ]
    for cp in outs_own[:2] + outs_twin[:2]:
        cp.start()
    for r in (1, 0):
        for j in range(2):
            for h in range(heads_per):
                col = slice((j * heads_per + h) * DH, (j * heads_per + h + 1) * DH)
                grad = dqa[2 * r + j, :, h * rows:(h + 1) * rows] * inv_root
                dq_n[r, :, col] = grad.astype(BF16).T
        (outs_twin if r else outs_own)[2].start()

    for kv, out in enumerate((dpk_hbm, dpv_hbm)):
        total = own_part[kv]
        for name in ("m5", "m7", "m4"):
            msg[name, kv].wait_recv()
            total = total + rcv[names.index(name), kv].astype(F32)
        pg_n[kv] = total.astype(BF16).T
        twin_rows = pl.ds(pl.multiple_of((1 - c) * piece, piece), piece)
        outs_own.append(
            pltpu.make_async_copy(pg_n.at[kv, my_rows, :], out.at[0, :, ck], sem_ol.at[4 + kv])
        )
        outs_twin.append(
            to(
                pg_n.at[kv, twin_rows, :], out.at[0, :, ck],
                sem_os.at[4 + kv], sem_or.at[4 + kv], twin,
            )
        )
        outs_twin[-1].start()
        outs_own[-1].start()

    for cp in [att_own] + outs_own:
        cp.wait()
    for cp in [att_twin] + outs_twin:
        cp.wait()
    for cp in pair + stats + glens + list(ag.values()) + list(msg.values()):
        cp.wait_send()


def on_device(n_grp, queries, resp_keys, resp_values, prompt_keys, prompt_values, out_grad,
              lengths, rewards):
    rows = queries.shape[2]
    half_q = queries.shape[3] // 2
    half_k = resp_keys.shape[3] // 2
    heads_per = half_q // half_k
    piece = prompt_keys.shape[1]
    blk = 2 * piece
    width = heads_per * rows
    anywhere = pl.BlockSpec(memory_space=pl.ANY)
    scalar = pl.BlockSpec(memory_space=pltpu.SMEM)
    dma = pltpu.SemaphoreType.DMA
    vmem = pltpu.VMEM
    scratch = [
        vmem((2, rows, half_q), BF16), vmem((2, rows, half_q), BF16),
        vmem((2, rows, half_k), BF16), vmem((2, rows, half_k), BF16),
        vmem((8, 2, blk, half_k), BF16),
        vmem((4, DH, width), BF16), vmem((4, DH, width), BF16),
        vmem((9, 4, blk, width), BF16),
        vmem((9, 8, width), F32), vmem((8, width), F32), vmem((8, width), F32),
        vmem((4, DH, width), F32), vmem((4, DH, width), F32),
        vmem((4, blk, width), BF16), vmem((2, 8, width), F32),
        vmem((8, 128), jnp.int32), vmem((16, 8, 128), jnp.int32),
        vmem((8, 128), jnp.int32), vmem((n_grp, 8, 128), jnp.int32),
        vmem((7, 2, half_k, blk), BF16), vmem((7, 2, half_k, blk), BF16),
        vmem((2, half_k, blk), F32),
        vmem((2, rows, half_q), BF16), vmem((2, rows, half_q), BF16),
        vmem((2, 2, rows, half_k), BF16), vmem((2, blk, half_k), BF16),
        dma((6,)), dma((6,)), dma((6,)), dma((8, 2)), dma((8, 2)),
        dma((16,)), dma((16,)), dma((n_grp,)), dma((n_grp,)),
        dma((7, 2)), dma((7, 2)), dma((6,)), dma((6,)), dma((6,)),
    ]
    like = lambda a: jax.ShapeDtypeStruct(a.shape, a.dtype)
    return pl.pallas_call(
        lambda *refs: kernel(n_grp, heads_per, *refs),
        out_shape=(
            like(queries), like(queries), like(resp_keys), like(resp_values),
            like(prompt_keys), like(prompt_values),
        ),
        in_specs=[anywhere] * 6 + [scalar] * 2,
        out_specs=(anywhere,) * 6,
        scratch_shapes=scratch,
        compiler_params=pltpu.CompilerParams(
            collective_id=0, has_side_effects=True, vmem_limit_bytes=60 * 2**20
        ),
        name="grpo_attention",
    )(queries, resp_keys, resp_values, prompt_keys, prompt_values, out_grad, lengths, rewards)


def solution(mesh):
    n_grp = mesh.shape["grp"]
    wide = P("grp", "resp", None, None)
    tall = P("grp", "resp", None)
    return jax.shard_map(
        lambda *arrays: on_device(n_grp, *arrays),
        mesh=mesh,
        in_specs=(wide, wide, wide, tall, tall, wide, P("grp", "resp"), P("grp", "resp")),
        out_specs=(wide, wide, wide, wide, tall, tall),
        check_vma=False,
    )
```

time: 372 us -> 128 us (0.34); the launches traced: 367 us -> 128 us
  Pallas kernels: 0 us -> 120 us
  waiting for transfers between devices: 101 us -> 0 us
  matrix products: 100 us -> 0 us
  blocking collectives: 77.7 us -> 0 us
  local copies, waits for them, and re-layouts: 57.7 us -> 6.35 us
  between operations: 17.4 us -> 1.95 us
  other arithmetic: 12 us -> 0 us
    pallas_call x0 -> x1, Pallas kernels: none -> 120 us  [on_device(): pl.pallas_call(lambda *refs: kernel(n_grp, heads_per, *refs), out_shape=(...]
    dot_general x34 -> x0, matrix products: 100 us -> none  [the longest x5 35.5 us: weighted(): jnp.einsum('ghtn,ngd->ghtd', soft_low, value_heads, preferred_element_typ...]
    reduce_scatter x2 -> x0, waiting for transfers between devices: 99.9 us -> none  [the longest x1 64.7 us: on_device(): lax.psum_scatter(stacked_terms[0].reshape(prompt_total, key_width).astype...]
    psum x2 -> x0, blocking collectives: 77.7 us -> none  [the longest x1 68.7 us: on_device(): live_total = lax.psum(length_own, ('grp', 'resp'))]
    dynamic_slice x16 -> x0, local copies, waits for them, and re-layouts: 17.5 us -> none  [block_scan(): return lax.scan(advance, state_now, (key_blocks, value_blocks))[0]]
    reduce_sum x6 -> x0, other arithmetic: 11.8 us -> none  [the longest x4 6.93 us: total_step(): jnp.sum(jnp.exp(block_logits - new_max[..., None]), axis=-1)]
    convert_element_type x3 -> x0, local copies, waits for them, and re-layouts: 11.4 us -> none  [the longest x1 4.36 us: on_device(): stacked_terms[0].reshape(prompt_total, key_width).astype(jnp.bfloat16)]
    while x32 -> x0, local copies, waits for them, and re-layouts: 11.4 us -> none  [the longest x4 11.3 us: block_scan(): return lax.scan(advance, state_now, (key_blocks, value_blocks))[0]]
  transfers between devices with their start and end apart: 4 -> 0, of which waited for: 2 -> 0; matrix products, arithmetic and copies ran while one was open for 10% -> 0% of each run, Pallas kernels for 0% -> 0%
where the time goes in v1:
time: 128 us
  Pallas kernels  120 us (94%)
  local copies, waits for them, and re-layouts  6.35 us (5%)
  between operations  1.95 us (2%)
    pallas_call x1, Pallas kernels, on_device(): pl.pallas_call(lambda *refs: kernel(n_grp, heads_per, *refs), out_shape=(...  120 us
    unnamed x16, local copies, waits for them, and re-layouts  6.35 us

profile of v1, /device:TPU:1, one launch (start us, length us, event | category | flops | bytes accessed | tf_op | source)
XLA Modules:
  0.0 127.8 jit_solution(17230934196525488280)
XLA Ops:
  1.9 119.5 %grpo_attention.1 = (bf16[1,1,256,2560]{3,2,1,0:T(8,128)(2,1)}, bf16[1,1,256,2560]{3,2,1,0:T(8,128)(2,1)}, bf16[1,1,256,512]{3,2,1,0:T(8,128)(2,1)}, bf16[1,1,25...) custom-call(bf16[1,1,256,2560]{3,2,1,0:T(8,128)(2,1)} %refs_0_.1, ...), custom_call_target="tpu_custom_call" | custom-call | tf_op jit(solution)/shard_map/grpo_attention/pallas_call | solution.py:431
  121.5 0.0 copy-start
  121.5 2.6 %copy.22 = bf16[1,1,256,2560]{3,2,1,0:T(8,128)(2,1)} copy(bf16[1,1,256,2560]{3,2,1,0:T(8,128)(2,1)} %get-tuple-element.12) | data formatting | bytes 2621440
  124.0 0.0 copy-done
  124.0 0.0 copy-start.2
  124.0 0.0 copy-start.1
  124.0 0.0 copy-start.4
  124.1 1.1 copy.23
  125.1 0.0 copy-done.2
  125.1 0.0 copy-start.3
  125.1 0.7 copy.24
  125.8 0.0 copy-done.1
  125.8 0.7 copy.25
  126.5 0.0 copy-done.4
  126.5 0.7 copy.26
  127.2 0.0 copy-done.3
  127.2 0.7 copy.27
Async XLA Ops:
  121.5 2.6 %copy-start = (bf16[1,1,256,2560]{3,2,1,0:T(8,128)(2,1)S(1)}, bf16[1,1,256,2560]{3,2,1,0:T(8,128)(2,1)}, u32[]{:S(2)}) copy-start(bf16[1,1,256,2560]{3,2,1,0:T(8,128)(2,1)} %get-tuple-element.13) | copy-start | bytes 3932164
  124.0 1.1 copy-start.2
  124.0 1.8 %copy-start.1 = (bf16[1,1,256,512]{3,2,1,0:T(8,128)(2,1)S(1)}, bf16[1,1,256,512]{3,2,1,0:T(8,128)(2,1)}, u32[]{:S(2)}) copy-start(bf16[1,1,256,512]{3,2,1,0:T(8,128)(2,1)} %get-tuple-element.15) | copy-start | bytes 786436
  124.0 2.5 %copy-start.4 = (bf16[1,128,512]{2,1,0:T(8,128)(2,1)S(1)}, bf16[1,128,512]{2,1,0:T(8,128)(2,1)}, u32[]{:S(2)}) copy-start(bf16[1,128,512]{2,1,0:T(8,128)(2,1)} %get-tuple-element.16) | copy-start | bytes 393220
  125.1 2.1 %copy-start.3 = (bf16[1,128,512]{2,1,0:T(8,128)(2,1)S(1)}, bf16[1,128,512]{2,1,0:T(8,128)(2,1)}, u32[]{:S(2)}) copy-start(bf16[1,128,512]{2,1,0:T(8,128)(2,1)} %get-tuple-element.17) | copy-start | bytes 393220

commit v2 on v1

--- a/solution.py
+++ b/solution.py
@@ -27,7 +27,7 @@
 def kernel(
     n_grp, heads_per, q_hbm, rk_hbm, rv_hbm, pk_hbm, pv_hbm, og_hbm, len_ref, rew_ref,
     att_hbm, dq_hbm, drk_hbm, drv_hbm, dpk_hbm, dpv_hbm,
-    qn, gn, rkn, rvn, kvn, qT, gT, e_st, m_st, m_cur, l_cur, acc, dqa, ds, aux,
+    qn, gn, rkn, rvn, kvn, qT, q2, gT, e_st, m_st, m_cur, l_cur, acc, dqa, aux,
     stat_out, stat_in, glen_out, glen_in, snd, rcv, own_part, att_n, dq_n, rg_n, pg_n,
     sem_l, sem_ps, sem_pr, sem_as, sem_ar, sem_ss, sem_sr, sem_gs, sem_gr,
     sem_ms, sem_mr, sem_ol, sem_os, sem_or,
@@ -135,33 +135,64 @@
                     r, :, (j * heads_per + h) * DH:(j * heads_per + h + 1) * DH
                 ].T
 
-    def forward(k, vt, u, block, first):
-        for h in range(heads_per):
-            cols = slice(h * rows, (h + 1) * rows)
-            s = nn(k, qT[u, :, cols])
+    def split_queries(r):
+        for u in (2 * r, 2 * r + 1):
+            for h in range(heads_per):
+                cols = slice(h * rows, (h + 1) * rows)
+                full = qT[u, :, cols].astype(F32) * scale2
+                high = full.astype(BF16)
+                q2[u, 0:DH, cols] = high
+                q2[u, DH:2 * DH, cols] = (full - high.astype(F32)).astype(BF16)
+
+    ones = jnp.ones((16, blk), BF16)
+
+    def forward(units, keys, values, block, first):
+        keys = {u: jnp.concatenate([k, k], axis=1) for u, k in keys.items()}
+        values = {u: jnp.concatenate([v.T, ones], axis=0) for u, v in values.items()}
+        todo = [(u, slice(h * rows, (h + 1) * rows)) for u in units for h in range(heads_per)]
+        logits, lows = {}, {}
+
+        def start(i):
+            u, cols = todo[i]
+            logits[i] = nn(keys[u], q2[u, :, cols])
+
+        def finish(i):
+            u, cols = todo[i]
+            low, alpha = lows.pop(i)
+            part = nn(values[u], low)
+            if first:
+                l_cur[u:u + 1, cols] = part[DH:DH + 1]
+                acc[u, :, cols] = part[0:DH]
+            else:
+                l_cur[u:u + 1, cols] = l_cur[u:u + 1, cols] * alpha + part[DH:DH + 1]
+                acc[u, :, cols] = acc[u, :, cols] * alpha + part[0:DH]
+
+        for i in range(3):
+            start(i)
+        for i, (u, cols) in enumerate(todo):
+            if i + 3 < len(todo):
+                start(i + 3)
+            s = logits.pop(i)
             if first:
                 seen = lax.broadcasted_iota(jnp.int32, s.shape, 0) <= (
                     lax.broadcasted_iota(jnp.int32, s.shape, 1)
                 )
                 s = jnp.where(seen, s, -jnp.inf)
                 m_new = jnp.max(s, axis=0, keepdims=True)
+                alpha = None
             else:
                 m_old = m_cur[u:u + 1, cols]
                 m_new = jnp.maximum(m_old, jnp.max(s, axis=0, keepdims=True))
-            e = jnp.exp2(s * scale2 - m_new * scale2)
-            total = jnp.sum(e, axis=0, keepdims=True)
-            low = e.astype(BF16)
+                alpha = jnp.exp2(m_old - m_new)
+            low = jnp.exp2(s - m_new).astype(BF16)
             e_st[block, u, :, cols] = low
-            part = nn(vt, low)
-            if first:
-                l_cur[u:u + 1, cols] = total
-                acc[u, :, cols] = part
-            else:
-                alpha = jnp.exp2((m_old - m_new) * scale2)
-                l_cur[u:u + 1, cols] = l_cur[u:u + 1, cols] * alpha + total
-                acc[u, :, cols] = acc[u, :, cols] * alpha + part
             m_cur[u:u + 1, cols] = m_new
             m_st[block, u:u + 1, cols] = m_new
+            lows[i] = (low, alpha)
+            if i >= 2:
+                finish(i - 2)
+        for i in sorted(lows):
+            finish(i)
 
     n_blocks = 8
     for r in range(2):
@@ -172,9 +203,18 @@
             for i in (2, 3, 4):
                 pair[i].wait_recv()
         turn(qn, qT, r)
-        for j in range(2):
-            heads = slice(j * DH, (j + 1) * DH)
-            forward(rkn[r, :, heads], rvn[r, :, heads].T, 2 * r + j, n_blocks, True)
+        split_queries(r)
+        units = (2 * r, 2 * r + 1)
+        forward(
+            units,
+            {u: rkn[r, :, (u % 2) * DH:(u % 2 + 1) * DH] for u in units},
+            {u: rvn[r, :, (u % 2) * DH:(u % 2 + 1) * DH] for u in units},
+            n_blocks, True,
+        )
+    local[5].wait()
+    pair[5].wait_recv()
+    for r in range(2):
+        turn(gn, gT, r)
 
     for cp in stats:
         cp.wait_recv()
@@ -230,12 +270,13 @@
         def _():
             pass_on([(ZYY, 0), (ZYY, 1)], [])
 
-        for j in range(2):
-            heads = slice(j * DH, (j + 1) * DH)
-            k = kvn[step, 0, :, heads]
-            vt = kvn[step, 1, :, heads].T
-            for r in range(2):
-                forward(k, vt, 2 * r + j, step, False)
+        order = (0, 2, 1, 3)
+        forward(
+            order,
+            {u: kvn[step, 0, :, (u % 2) * DH:(u % 2 + 1) * DH] for u in order},
+            {u: kvn[step, 1, :, (u % 2) * DH:(u % 2 + 1) * DH] for u in order},
+            step, False,
+        )
 
     for cp in glens:
         cp.wait_recv()
@@ -248,10 +289,7 @@
     variance = (n_resp * sum_two - sum_one * sum_one) / (n_resp * n_resp)
     spread = jnp.maximum(jnp.sqrt(variance), 1.0)
     norm = (n_grp * n_resp * rows) / live.astype(F32)
-    local[5].wait()
-    pair[5].wait_recv()
     for r in range(2):
-        turn(gn, gT, r)
         length = stat_out[0:1, :] if r == 0 else stat_in[1, 0:1, :]
         reward = stat_out[1:2, :] if r == 0 else stat_in[1, 1:2, :]
         strength = (reward.astype(F32) - mean) / spread * norm
@@ -284,20 +322,43 @@
     att_own.start()
     att_twin.start()
 
-    def backward(k, v, kt, u, block, tmp):
-        scaled = []
-        for h in range(heads_per):
-            cols = slice(h * rows, (h + 1) * rows)
-            m_fin = m_cur[u:u + 1, cols]
-            factor = jnp.exp2((m_st[block, u:u + 1, cols] - m_fin) * scale2) * aux[0, u:u + 1, cols]
-            g = (gT[u, :, cols].astype(F32) * factor).astype(BF16)
-            scaled.append(g)
-            d = nn(v, g) - factor * aux[1, u:u + 1, cols]
-            low = (e_st[block, u, :, cols].astype(F32) * d).astype(BF16)
-            ds[tmp, :, cols] = low
-            dqa[u, :, cols] = dqa[u, :, cols] + nn(kt, low)
-        g_all = jnp.concatenate(scaled, axis=1)
-        return nt(qT[u], ds[tmp]) * inv_root, nt(g_all, e_st[block, u])
+    def backward(units, keys, values, block, place):
+        flat = {u: k.T for u, k in keys.items()}
+        todo = [(u, h, slice(h * rows, (h + 1) * rows)) for u in units for h in range(heads_per)]
+        scaled, shift, dots, lows, sums = {}, {}, {}, {}, {}
+
+        def start(i):
+            u, h, cols = todo[i]
+            factor = jnp.exp2(m_st[block, u:u + 1, cols] - m_cur[u:u + 1, cols])
+            factor = factor * aux[0, u:u + 1, cols]
+            scaled[i] = (gT[u, :, cols].astype(F32) * factor).astype(BF16)
+            shift[i] = factor * aux[1, u:u + 1, cols]
+            dots[i] = nn(values[u], scaled[i])
+
+        def add(key, term):
+            sums[key] = sums[key] + term if key in sums else term
+
+        def finish(i):
+            u, h, cols = todo[i]
+            low = lows.pop(i)
+            col = (u % 2) * heads_per + h
+            dqa[u, :, cols] = dqa[u, :, cols] + nn(flat[u], low)
+            add((place(u), 0), nn(low, qn[u // 2, :, col * DH:(col + 1) * DH]))
+            add((place(u), 1), nt(scaled.pop(i), e_st[block, u, :, cols]))
+
+        for i in range(2):
+            start(i)
+        for i, (u, h, cols) in enumerate(todo):
+            if i + 2 < len(todo):
+                start(i + 2)
+            d = dots.pop(i) - shift.pop(i)
+            lows[i] = (e_st[block, u, :, cols].astype(F32) * d).astype(BF16)
+            if i >= 1:
+                finish(i - 1)
+        finish(len(todo) - 1)
+        return {
+            key: term.T * inv_root if key[1] == 0 else term for key, term in sums.items()
+        }
 
     names = ("m1", "m6", "m3", "m2", "m7", "m5", "m4")
     route = {
@@ -319,15 +380,15 @@
     @pl.loop(0, n_blocks)
     def backward_step(step):
         block = n_blocks - 1 - step
-        for j in range(2):
-            heads = slice(j * DH, (j + 1) * DH)
-            k = kvn[block, 0, :, heads]
-            v = kvn[block, 1, :, heads]
-            kt = k.T
-            first = backward(k, v, kt, j, block, 2 * j)
-            second = backward(k, v, kt, 2 + j, block, 2 * j + 1)
-            own_part[0, heads, :] = first[0] + second[0]
-            own_part[1, heads, :] = first[1] + second[1]
+        order = (0, 2, 1, 3)
+        sums = backward(
+            order,
+            {u: kvn[block, 0, :, (u % 2) * DH:(u % 2 + 1) * DH] for u in order},
+            {u: kvn[block, 1, :, (u % 2) * DH:(u % 2 + 1) * DH] for u in order},
+            block, lambda u: u % 2,
+        )
+        for (j, kv), term in sums.items():
+            own_part[kv, j * DH:(j + 1) * DH, :] = term
 
         for n, name in enumerate(names):
             @pl.when(step == n)
@@ -340,14 +401,15 @@
                     snd[n, kv] = total.astype(BF16)
                     msg[name, kv].start()
 
-    for r in range(2):
-        for j in range(2):
-            heads = slice(j * DH, (j + 1) * DH)
-            k = rkn[r, :, heads]
-            v = rvn[r, :, heads]
-            grad_k, grad_v = backward(k, v, k.T, 2 * r + j, n_blocks, j)
-            rg_n[r, 0, :, heads] = grad_k.astype(BF16).T
-            rg_n[r, 1, :, heads] = grad_v.astype(BF16).T
+    units = (0, 1, 2, 3)
+    sums = backward(
+        units,
+        {u: rkn[u // 2, :, (u % 2) * DH:(u % 2 + 1) * DH] for u in units},
+        {u: rvn[u // 2, :, (u % 2) * DH:(u % 2 + 1) * DH] for u in units},
+        n_blocks, lambda u: u,
+    )
+    for (u, kv), term in sums.items():
+        rg_n[u // 2, kv, :, (u % 2) * DH:(u % 2 + 1) * DH] = term.astype(BF16).T
     outs_own = [
         pltpu.make_async_copy(rg_n.at[0, 0], drk_hbm.at[0, 0, :, ck], sem_ol.at[1]),
         pltpu.make_async_copy(rg_n.at[0, 1], drv_hbm.at[0, 0, :, ck], sem_ol.at[2]),
@@ -412,11 +474,11 @@
         vmem((2, rows, half_q), BF16), vmem((2, rows, half_q), BF16),
         vmem((2, rows, half_k), BF16), vmem((2, rows, half_k), BF16),
         vmem((8, 2, blk, half_k), BF16),
-        vmem((4, DH, width), BF16), vmem((4, DH, width), BF16),
+        vmem((4, DH, width), BF16), vmem((4, 2 * DH, width), BF16), vmem((4, DH, width), BF16),
         vmem((9, 4, blk, width), BF16),
         vmem((9, 8, width), F32), vmem((8, width), F32), vmem((8, width), F32),
         vmem((4, DH, width), F32), vmem((4, DH, width), F32),
-        vmem((4, blk, width), BF16), vmem((2, 8, width), F32),
+        vmem((2, 8, width), F32),
         vmem((8, 128), jnp.int32), vmem((16, 8, 128), jnp.int32),
         vmem((8, 128), jnp.int32), vmem((n_grp, 8, 128), jnp.int32),
         vmem((7, 2, half_k, blk), BF16), vmem((7, 2, half_k, blk), BF16),

time: 128 us -> 72.5 us (0.57)
  Pallas kernels: 120 us -> 64.1 us
    pallas_call x1, Pallas kernels: 120 us -> 64.1 us  [on_device(): pl.pallas_call(lambda *refs: kernel(n_grp, heads_per, *refs), out_shape=(...]
where the time goes in v2:
time: 72.5 us; the launch traced here: 72.4 us
  Pallas kernels  64.1 us (88%)
  local copies, waits for them, and re-layouts  6.35 us (9%)
  between operations  1.95 us (3%)
    pallas_call x1, Pallas kernels, on_device(): pl.pallas_call(lambda *refs: kernel(n_grp, heads_per, *refs), out_shape=(...  64.1 us
    unnamed x16, local copies, waits for them, and re-layouts  6.35 us

profile of v2, /device:TPU:1, one launch (start us, length us, event | category | flops | bytes accessed | tf_op | source)
XLA Modules:
  0.0 72.4 jit_solution(13771055231328792486)
XLA Ops:
  1.9 64.1 %grpo_attention.1 = (bf16[1,1,256,2560]{3,2,1,0:T(8,128)(2,1)}, bf16[1,1,256,2560]{3,2,1,0:T(8,128)(2,1)}, bf16[1,1,256,512]{3,2,1,0:T(8,128)(2,1)}, bf16[1,1,25...) custom-call(bf16[1,1,256,2560]{3,2,1,0:T(8,128)(2,1)} %refs_0_.1, ...), custom_call_target="tpu_custom_call" | custom-call | tf_op jit(solution)/shard_map/grpo_attention/pallas_call | solution.py:493
  66.0 0.0 copy-start
  66.0 2.6 %copy.22 = bf16[1,1,256,2560]{3,2,1,0:T(8,128)(2,1)} copy(bf16[1,1,256,2560]{3,2,1,0:T(8,128)(2,1)} %get-tuple-element.12) | data formatting | bytes 2621440
  68.6 0.0 copy-done
  68.6 0.0 copy-start.2
  68.6 0.0 copy-start.1
  68.6 0.0 copy-start.4
  68.6 1.1 %copy.23 = bf16[1,1,256,2560]{3,2,1,0:T(8,128)(2,1)} copy(bf16[1,1,256,2560]{3,2,1,0:T(8,128)(2,1)S(1)} %copy-done) | data formatting | bytes 2621440
  69.6 0.0 copy-done.2
  69.6 0.0 copy-start.3
  69.6 0.7 copy.24
  70.3 0.0 copy-done.1
  70.3 0.7 copy.25
  71.1 0.0 copy-done.4
  71.1 0.7 copy.26
  71.7 0.0 copy-done.3
  71.7 0.7 copy.27
Async XLA Ops:
  66.0 2.6 %copy-start = (bf16[1,1,256,2560]{3,2,1,0:T(8,128)(2,1)S(1)}, bf16[1,1,256,2560]{3,2,1,0:T(8,128)(2,1)}, u32[]{:S(2)}) copy-start(bf16[1,1,256,2560]{3,2,1,0:T(8,128)(2,1)} %get-tuple-element.13) | copy-start | bytes 3932164
  68.6 1.1 %copy-start.2 = (bf16[1,1,256,512]{3,2,1,0:T(8,128)(2,1)S(1)}, bf16[1,1,256,512]{3,2,1,0:T(8,128)(2,1)}, u32[]{:S(2)}) copy-start(bf16[1,1,256,512]{3,2,1,0:T(8,128)(2,1)} %get-tuple-element.14) | copy-start | bytes 786436
  68.6 1.8 %copy-start.1 = (bf16[1,1,256,512]{3,2,1,0:T(8,128)(2,1)S(1)}, bf16[1,1,256,512]{3,2,1,0:T(8,128)(2,1)}, u32[]{:S(2)}) copy-start(bf16[1,1,256,512]{3,2,1,0:T(8,128)(2,1)} %get-tuple-element.15) | copy-start | bytes 786436
  68.6 2.5 %copy-start.4 = (bf16[1,128,512]{2,1,0:T(8,128)(2,1)S(1)}, bf16[1,128,512]{2,1,0:T(8,128)(2,1)}, u32[]{:S(2)}) copy-start(bf16[1,128,512]{2,1,0:T(8,128)(2,1)} %get-tuple-element.16) | copy-start | bytes 393220
  69.6 2.1 %copy-start.3 = (bf16[1,128,512]{2,1,0:T(8,128)(2,1)S(1)}, bf16[1,128,512]{2,1,0:T(8,128)(2,1)}, u32[]{:S(2)}) copy-start(bf16[1,128,512]{2,1,0:T(8,128)(2,1)} %get-tuple-element.17) | copy-start | bytes 393220

commit v3 on v2

--- a/solution.py
+++ b/solution.py
@@ -25,11 +25,11 @@
 
 
 def kernel(
-    n_grp, heads_per, q_hbm, rk_hbm, rv_hbm, pk_hbm, pv_hbm, og_hbm, len_ref, rew_ref,
+    n_grp, heads_per, q_hbm, rk_hbm, rv_hbm, pk_hbm, pv_hbm, og_hbm, len_hbm, rew_hbm,
     att_hbm, dq_hbm, drk_hbm, drv_hbm, dpk_hbm, dpv_hbm,
-    qn, gn, rkn, rvn, kvn, qT, q2, gT, e_st, m_st, m_cur, l_cur, acc, dqa, aux,
-    stat_out, stat_in, glen_out, glen_in, snd, rcv, own_part, att_n, dq_n, rg_n, pg_n,
-    sem_l, sem_ps, sem_pr, sem_as, sem_ar, sem_ss, sem_sr, sem_gs, sem_gr,
+    len_ref, rew_ref, qn, gn, rkn, rvn, kvn, qT, q2, gT, e_st, m_st, m_cur, l_cur, acc, dqa, aux,
+    stat_out, stat_in, snd, rcv, own_part, att_n, dq_n, rg_n, pg_n,
+    sem_l, sem_ps, sem_pr, sem_as, sem_ar, sem_bs, sem_br, sem_ss, sem_sr,
     sem_ms, sem_mr, sem_ol, sem_os, sem_or,
 ):
     rows = qn.shape[1]
@@ -68,65 +68,27 @@
         pltpu.make_async_copy(rk_hbm.at[0, 0, :, ck], rkn.at[0], sem_l.at[3]),
         pltpu.make_async_copy(rv_hbm.at[0, 0, :, ck], rvn.at[0], sem_l.at[4]),
         pltpu.make_async_copy(og_hbm.at[0, 0, :, cq], gn.at[0], sem_l.at[5]),
+        pltpu.make_async_copy(len_hbm, len_ref, sem_l.at[6]),
+        pltpu.make_async_copy(rew_hbm, rew_ref, sem_l.at[7]),
     ]
     for cp in local:
         cp.start()
 
-    row_id = lax.broadcasted_iota(jnp.int32, (8, 128), 0)
-    stat_out[...] = jnp.where(row_id == 0, len_ref[0, 0], rew_ref[0, 0])
-
-    others = [
-        (dz, dy, dc) for dz in range(2) for dy in range(4) for dc in range(2) if dz or dy or dc
-    ]
+    twin = at(0, 0, 1)
+    z_to, up, down = at(1, 0, 0), at(0, 1, 0), at(0, 3, 0)
+    ring = min(4, n_grp)
+    base = (grp // ring) * ring
+    x_up = {"grp": base + (grp - base + 1) % ring}
+    x_down = {"grp": base + (grp - base + ring - 1) % ring}
+    across = {"grp": (grp + ring) % n_grp}
+    friends = [twin, z_to, up, down]
+    if ring == 4:
+        friends += [x_up, x_down]
+    if n_grp > ring:
+        friends.append(across)
     barrier = pltpu.get_barrier_semaphore()
-    for dz, dy, dc in others:
-        pl.semaphore_signal(barrier, inc=1, device_id=at(dz, dy, dc), device_id_type=MESH)
-    for dg in range(1, n_grp):
-        pl.semaphore_signal(
-            barrier, inc=1, device_id={"grp": (grp + dg) % n_grp}, device_id_type=MESH
-        )
-    pl.semaphore_wait(barrier, len(others) + n_grp - 1)
-
-    twin = at(0, 0, 1)
-    pair = [
-        to(pk_hbm.at[0, :, ok], kvn.at[OWN, 0, my_rows, :], sem_ps.at[0], sem_pr.at[0], twin),
-        to(pv_hbm.at[0, :, ok], kvn.at[OWN, 1, my_rows, :], sem_ps.at[1], sem_pr.at[1], twin),
-        to(q_hbm.at[0, 0, :, oq], qn.at[1], sem_ps.at[2], sem_pr.at[2], twin),
-        to(rk_hbm.at[0, 0, :, ok], rkn.at[1], sem_ps.at[3], sem_pr.at[3], twin),
-        to(rv_hbm.at[0, 0, :, ok], rvn.at[1], sem_ps.at[4], sem_pr.at[4], twin),
-        to(og_hbm.at[0, 0, :, oq], gn.at[1], sem_ps.at[5], sem_pr.at[5], twin),
-    ]
-    for cp in pair:
-        cp.start()
-
-    z_to, up, down = at(1, 0, 0), at(0, 1, 0), at(0, 3, 0)
-    ag_plan = (
-        (OWN, ZZ, 0, z_to), (OWN, YM, 0, up), (OWN, YP, 0, down),
-        (OWN, ZZ, 1, z_to), (OWN, YM, 1, up), (OWN, YP, 1, down),
-        (YM, YY, 0, up), (YM, ZYM, 0, z_to), (YM, ZYM, 1, z_to),
-        (YP, YY, 1, down), (ZZ, ZYP, 0, down), (ZZ, ZYP, 1, down),
-        (ZYM, ZYY, 0, up), (ZYM, ZYY, 1, up),
-    )
-    ag = {}
-    for src, dst, kv, target in ag_plan:
-        ag[dst, kv] = to(
-            kvn.at[src, kv], kvn.at[dst, kv], sem_as.at[dst, kv], sem_ar.at[dst, kv], target
-        )
-
-    for i in (0, 1):
-        local[i].wait()
-        pair[i].wait_recv()
-    for kv in (0, 1):
-        for dst in (ZZ, YM, YP):
-            ag[dst, kv].start()
-
-    stats = []
-    for n, (dz, dy, dc) in enumerate(others):
-        slot = ((-dz) % 2) * 8 + ((-dy) % 4) * 2 + dc
-        stats.append(
-            to(stat_out, stat_in.at[slot], sem_ss.at[slot], sem_sr.at[slot], at(dz, dy, dc))
-        )
-        stats[-1].start()
+    for friend in friends:
+        pl.semaphore_signal(barrier, inc=1, device_id=friend, device_id_type=MESH)
 
     def turn(src, dst, r):
         for j in range(2):
@@ -194,14 +156,7 @@
         for i in sorted(lows):
             finish(i)
 
-    n_blocks = 8
-    for r in range(2):
-        if r == 0:
-            for i in (2, 3, 4):
-                local[i].wait()
-        else:
-            for i in (2, 3, 4):
-                pair[i].wait_recv()
+    def own_block(r):
         turn(qn, qT, r)
         split_queries(r)
         units = (2 * r, 2 * r + 1)
@@ -211,37 +166,113 @@
             {u: rvn[r, :, (u % 2) * DH:(u % 2 + 1) * DH] for u in units},
             n_blocks, True,
         )
+
+    n_blocks = 8
+    for i in (2, 3, 4):
+        local[i].wait()
+    own_block(0)
+
+    pl.semaphore_wait(barrier, len(friends))
+
+    pair = [
+        to(pk_hbm.at[0, :, ok], kvn.at[OWN, 0, my_rows, :], sem_ps.at[0], sem_pr.at[0], twin),
+        to(pv_hbm.at[0, :, ok], kvn.at[OWN, 1, my_rows, :], sem_ps.at[1], sem_pr.at[1], twin),
+        to(q_hbm.at[0, 0, :, oq], qn.at[1], sem_ps.at[2], sem_pr.at[2], twin),
+        to(rk_hbm.at[0, 0, :, ok], rkn.at[1], sem_ps.at[3], sem_pr.at[3], twin),
+        to(rv_hbm.at[0, 0, :, ok], rvn.at[1], sem_ps.at[4], sem_pr.at[4], twin),
+        to(og_hbm.at[0, 0, :, oq], gn.at[1], sem_ps.at[5], sem_pr.at[5], twin),
+    ]
+    for cp in pair:
+        cp.start()
+
+    twin_rows = pl.ds(pl.multiple_of((1 - c) * piece, piece), piece)
+    ag = {}
+    for kv in (0, 1):
+        for dst, target in ((YM, up), (YP, down), (ZZ, z_to)):
+            ag[dst, kv] = [
+                to(
+                    kvn.at[OWN, kv, part, :], kvn.at[dst, kv, part, :],
+                    s_sem.at[dst, kv], r_sem.at[dst, kv], target,
+                )
+                for part, s_sem, r_sem in (
+                    (my_rows, sem_as, sem_ar), (twin_rows, sem_bs, sem_br),
+                )
+            ]
+    ag_plan = (
+        (YM, YY, 0, up), (YM, ZYM, 0, z_to), (YM, ZYM, 1, z_to),
+        (YP, YY, 1, down), (ZZ, ZYP, 0, down), (ZZ, ZYP, 1, down),
+        (ZYM, ZYY, 0, up), (ZYM, ZYY, 1, up),
+    )
+    for src, dst, kv, target in ag_plan:
+        ag[dst, kv] = [
+            to(kvn.at[src, kv], kvn.at[dst, kv], sem_as.at[dst, kv], sem_ar.at[dst, kv], target)
+        ]
+
+    for half in (0, 1):
+        for kv in (0, 1):
+            if half == 0:
+                local[kv].wait()
+            else:
+                pair[kv].wait_recv()
+            for dst in (YM, YP, ZZ):
+                ag[dst, kv][half].start()
+
+
+    hops = [((twin,), False), ((z_to,), False), ((up, down), False), ((up,), True)]
+    if ring == 4:
+        hops += [((x_up, x_down), False), ((x_up,), True)]
+    if n_grp > ring:
+        hops.append(((across,), False))
+
+    def hop_copies(n):
+        targets, relay = hops[n]
+        src = stat_in.at[n - 1, 1] if relay else stat_out.at[n]
+        copies = []
+        for i, target in enumerate(targets):
+            slot = 1 - i if len(targets) == 2 else 0
+            copies.append(
+                to(src, stat_in.at[n, slot], sem_ss.at[n, slot], sem_sr.at[n, slot], target)
+            )
+        return copies
+
+    def hop_start(n):
+        for cp in hop_copies(n):
+            cp.start()
+
+    def hop_end(n):
+        for cp in hop_copies(n):
+            cp.wait_recv()
+        total = stat_out[n]
+        for slot in range(len(hops[n][0])):
+            total = total + stat_in[n, slot]
+        stat_out[n + 1] = total
+
+    local[6].wait()
+    local[7].wait()
+    row_id = lax.broadcasted_iota(jnp.int32, (8, 128), 0)
+    reward_own = rew_ref[0, 0]
+    stat_out[0] = jnp.where(
+        row_id == 0, len_ref[0, 0], jnp.where(row_id == 1, reward_own, reward_own * reward_own)
+    )
+    hop_start(0)
+
+    for i in (2, 3, 4):
+        pair[i].wait_recv()
+    own_block(1)
     local[5].wait()
     pair[5].wait_recv()
     for r in range(2):
         turn(gn, gT, r)
-
-    for cp in stats:
-        cp.wait_recv()
-    sum_one = stat_out[1:2, :]
-    sum_two = sum_one * sum_one
-    live = stat_out[0:1, :]
-    for slot in range(1, 16):
-        one = stat_in[slot, 1:2, :]
-        sum_one = sum_one + one
-        sum_two = sum_two + one * one
-        live = live + stat_in[slot, 0:1, :]
-    glen_out[...] = jnp.broadcast_to(live, (8, 128))
-    glens = []
-    for dg in range(1, n_grp):
-        glens.append(
-            to(
-                glen_out, glen_in.at[n_grp - dg], sem_gs.at[n_grp - dg], sem_gr.at[n_grp - dg],
-                {"grp": (grp + dg) % n_grp},
-            )
-        )
-        glens[-1].start()
+    hop_end(0)
+    hop_start(1)
 
     def pass_on(waits, starts):
         for key in waits:
-            ag[key].wait_recv()
+            for cp in ag[key]:
+                cp.wait_recv()
         for key in starts:
-            ag[key].start()
+            for cp in ag[key]:
+                cp.start()
 
     @pl.loop(0, n_blocks)
     def forward_step(step):
@@ -253,9 +284,12 @@
             pass_on([(YP, 0), (YP, 1)], [(YY, 1)])
             pass_on([(ZZ, 1)], [(ZYP, 1)])
 
+        @pl.when(step == 3)
+        def _():
+            pass_on([(ZYM, 0)], [(ZYY, 0)])
+
         @pl.when(step == 4)
         def _():
-            pass_on([(ZYM, 0)], [(ZYY, 0)])
             pass_on([(ZYM, 1)], [(ZYY, 1)])
 
         @pl.when(step == 5)
@@ -269,6 +303,13 @@
         @pl.when(step == 7)
         def _():
             pass_on([(ZYY, 0), (ZYY, 1)], [])
+
+        for n in range(1, len(hops)):
+            @pl.when(step == n)
+            def _():
+                hop_end(n)
+                if n + 1 < len(hops):
+                    hop_start(n + 1)
 
         order = (0, 2, 1, 3)
         forward(
@@ -278,10 +319,10 @@
             step, False,
         )
 
-    for cp in glens:
-        cp.wait_recv()
-    for slot in range(1, n_grp):
-        live = live + glen_in[slot, 0:1, :]
+    resp_hops = 4
+    sum_one = stat_out[resp_hops, 1:2, :]
+    sum_two = stat_out[resp_hops, 2:3, :]
+    live = stat_out[len(hops), 0:1, :]
     n_resp = 16
     sum_one = sum_one.astype(F32)
     sum_two = sum_two.astype(F32)
@@ -290,8 +331,8 @@
     spread = jnp.maximum(jnp.sqrt(variance), 1.0)
     norm = (n_grp * n_resp * rows) / live.astype(F32)
     for r in range(2):
-        length = stat_out[0:1, :] if r == 0 else stat_in[1, 0:1, :]
-        reward = stat_out[1:2, :] if r == 0 else stat_in[1, 1:2, :]
+        length = stat_out[0, 0:1, :] if r == 0 else stat_in[0, 0, 0:1, :]
+        reward = stat_out[0, 1:2, :] if r == 0 else stat_in[0, 0, 1:2, :]
         strength = (reward.astype(F32) - mean) / spread * norm
         weight = jnp.concatenate(
             [
@@ -308,19 +349,13 @@
                 cols = slice(h * rows, (h + 1) * rows)
                 inv = 1.0 / l_cur[u:u + 1, cols]
                 out = (acc[u, :, cols] * inv).astype(BF16)
-                col = slice((j * heads_per + h) * DH, (j * heads_per + h + 1) * DH)
-                att_n[r, :, col] = out.T
+                q2[u, 0:DH, cols] = out
                 delta = jnp.sum(
                     out.astype(F32) * gT[u, :, cols].astype(F32), axis=0, keepdims=True
                 )
                 aux[0, u:u + 1, cols] = inv * weight
                 aux[1, u:u + 1, cols] = delta
                 dqa[u, :, cols] = jnp.zeros((DH, rows), F32)
-
-    att_own = pltpu.make_async_copy(att_n.at[0], att_hbm.at[0, 0, :, cq], sem_ol.at[0])
-    att_twin = to(att_n.at[1], att_hbm.at[0, 0, :, cq], sem_os.at[0], sem_or.at[0], twin)
-    att_own.start()
-    att_twin.start()
 
     def backward(units, keys, values, block, place):
         flat = {u: k.T for u, k in keys.items()}
@@ -387,6 +422,15 @@
             {u: kvn[block, 1, :, (u % 2) * DH:(u % 2 + 1) * DH] for u in order},
             block, lambda u: u % 2,
         )
+        total_heads = 4 * heads_per
+        for i in range(3):
+            head = jnp.minimum(3 * step + i, total_heads - 1)
+            u = head // heads_per
+            h = head % heads_per
+            col = pl.multiple_of(((u % 2) * heads_per + h) * DH, DH)
+            att_n[u // 2, :, pl.ds(col, DH)] = q2[
+                u, 0:DH, pl.ds(pl.multiple_of(h * rows, rows), rows)
+            ].T
         for (j, kv), term in sums.items():
             own_part[kv, j * DH:(j + 1) * DH, :] = term
 
@@ -401,15 +445,11 @@
                     snd[n, kv] = total.astype(BF16)
                     msg[name, kv].start()
 
-    units = (0, 1, 2, 3)
-    sums = backward(
-        units,
-        {u: rkn[u // 2, :, (u % 2) * DH:(u % 2 + 1) * DH] for u in units},
-        {u: rvn[u // 2, :, (u % 2) * DH:(u % 2 + 1) * DH] for u in units},
-        n_blocks, lambda u: u,
-    )
-    for (u, kv), term in sums.items():
-        rg_n[u // 2, kv, :, (u % 2) * DH:(u % 2 + 1) * DH] = term.astype(BF16).T
+    att_own = pltpu.make_async_copy(att_n.at[0], att_hbm.at[0, 0, :, cq], sem_ol.at[0])
+    att_twin = to(att_n.at[1], att_hbm.at[0, 0, :, cq], sem_os.at[0], sem_or.at[0], twin)
+    att_own.start()
+    att_twin.start()
+
     outs_own = [
         pltpu.make_async_copy(rg_n.at[0, 0], drk_hbm.at[0, 0, :, ck], sem_ol.at[1]),
         pltpu.make_async_copy(rg_n.at[0, 1], drv_hbm.at[0, 0, :, ck], sem_ol.at[2]),
@@ -420,15 +460,23 @@
         to(rg_n.at[1, 1], drv_hbm.at[0, 0, :, ck], sem_os.at[2], sem_or.at[2], twin),
         to(dq_n.at[1], dq_hbm.at[0, 0, :, cq], sem_os.at[3], sem_or.at[3], twin),
     ]
-    for cp in outs_own[:2] + outs_twin[:2]:
-        cp.start()
     for r in (1, 0):
+        units = (2 * r, 2 * r + 1)
+        sums = backward(
+            units,
+            {u: rkn[r, :, (u % 2) * DH:(u % 2 + 1) * DH] for u in units},
+            {u: rvn[r, :, (u % 2) * DH:(u % 2 + 1) * DH] for u in units},
+            n_blocks, lambda u: u,
+        )
         for j in range(2):
             for h in range(heads_per):
                 col = slice((j * heads_per + h) * DH, (j * heads_per + h + 1) * DH)
                 grad = dqa[2 * r + j, :, h * rows:(h + 1) * rows] * inv_root
                 dq_n[r, :, col] = grad.astype(BF16).T
-        (outs_twin if r else outs_own)[2].start()
+        for (u, kv), term in sums.items():
+            rg_n[r, kv, :, (u % 2) * DH:(u % 2 + 1) * DH] = term.astype(BF16).T
+        for cp in outs_twin if r else outs_own:
+            cp.start()
 
     for kv, out in enumerate((dpk_hbm, dpv_hbm)):
         total = own_part[kv]
@@ -436,7 +484,6 @@
             msg[name, kv].wait_recv()
             total = total + rcv[names.index(name), kv].astype(F32)
         pg_n[kv] = total.astype(BF16).T
-        twin_rows = pl.ds(pl.multiple_of((1 - c) * piece, piece), piece)
         outs_own.append(
             pltpu.make_async_copy(pg_n.at[kv, my_rows, :], out.at[0, :, ck], sem_ol.at[4 + kv])
         )
@@ -453,8 +500,27 @@
         cp.wait()
     for cp in [att_twin] + outs_twin:
         cp.wait()
-    for cp in pair + stats + glens + list(ag.values()) + list(msg.values()):
+    stats = [cp for n in range(len(hops)) for cp in hop_copies(n)]
+    for cp in pair + stats + sum(ag.values(), []) + list(msg.values()):
         cp.wait_send()
+
+
+def finish(*refs):
+    ins, outs, sems = refs[:6], refs[6:12], refs[12]
+    copies = []
+    for src, dst in zip(ins, outs):
+        total = src.shape[-2]
+        pieces = 4 if src.shape[-1] > 1024 else 2
+        step = total // pieces
+        lead = (0,) * (len(src.shape) - 2)
+        for i in range(pieces):
+            part = lead + (pl.ds(i * step, step),)
+            copies.append(
+                pltpu.make_async_copy(src.at[part], dst.at[part], sems.at[len(copies)])
+            )
+            copies[-1].start()
+    for cp in copies:
+        cp.wait()
 
 
 def on_device(n_grp, queries, resp_keys, resp_values, prompt_keys, prompt_values, out_grad,
@@ -467,10 +533,10 @@
     blk = 2 * piece
     width = heads_per * rows
     anywhere = pl.BlockSpec(memory_space=pl.ANY)
-    scalar = pl.BlockSpec(memory_space=pltpu.SMEM)
     dma = pltpu.SemaphoreType.DMA
     vmem = pltpu.VMEM
     scratch = [
+        pltpu.SMEM((1, 1), jnp.int32), pltpu.SMEM((1, 1), jnp.int32),
         vmem((2, rows, half_q), BF16), vmem((2, rows, half_q), BF16),
         vmem((2, rows, half_k), BF16), vmem((2, rows, half_k), BF16),
         vmem((8, 2, blk, half_k), BF16),
@@ -479,24 +545,25 @@
         vmem((9, 8, width), F32), vmem((8, width), F32), vmem((8, width), F32),
         vmem((4, DH, width), F32), vmem((4, DH, width), F32),
         vmem((2, 8, width), F32),
-        vmem((8, 128), jnp.int32), vmem((16, 8, 128), jnp.int32),
-        vmem((8, 128), jnp.int32), vmem((n_grp, 8, 128), jnp.int32),
+        vmem((8, 8, 128), jnp.int32), vmem((8, 2, 8, 128), jnp.int32),
         vmem((7, 2, half_k, blk), BF16), vmem((7, 2, half_k, blk), BF16),
         vmem((2, half_k, blk), F32),
         vmem((2, rows, half_q), BF16), vmem((2, rows, half_q), BF16),
         vmem((2, 2, rows, half_k), BF16), vmem((2, blk, half_k), BF16),
-        dma((6,)), dma((6,)), dma((6,)), dma((8, 2)), dma((8, 2)),
-        dma((16,)), dma((16,)), dma((n_grp,)), dma((n_grp,)),
+        dma((8,)), dma((6,)), dma((6,)), dma((8, 2)), dma((8, 2)),
+        dma((8, 2)), dma((8, 2)),
+        dma((8, 2)), dma((8, 2)),
         dma((7, 2)), dma((7, 2)), dma((6,)), dma((6,)), dma((6,)),
     ]
     like = lambda a: jax.ShapeDtypeStruct(a.shape, a.dtype)
-    return pl.pallas_call(
+    shapes = (
+        like(queries), like(queries), like(resp_keys), like(resp_values),
+        like(prompt_keys), like(prompt_values),
+    )
+    results = pl.pallas_call(
         lambda *refs: kernel(n_grp, heads_per, *refs),
-        out_shape=(
-            like(queries), like(queries), like(resp_keys), like(resp_values),
-            like(prompt_keys), like(prompt_values),
-        ),
-        in_specs=[anywhere] * 6 + [scalar] * 2,
+        out_shape=shapes,
+        in_specs=[anywhere] * 6 + [pl.BlockSpec(memory_space=pltpu.HBM)] * 2,
         out_specs=(anywhere,) * 6,
         scratch_shapes=scratch,
         compiler_params=pltpu.CompilerParams(
@@ -504,6 +571,15 @@
         ),
         name="grpo_attention",
     )(queries, resp_keys, resp_values, prompt_keys, prompt_values, out_grad, lengths, rewards)
+    return pl.pallas_call(
+        finish,
+        out_shape=shapes,
+        in_specs=[anywhere] * 6,
+        out_specs=(anywhere,) * 6,
+        scratch_shapes=[dma((16,))],
+        compiler_params=pltpu.CompilerParams(vmem_limit_bytes=60 * 2**20),
+        name="write_results",
+    )(*results)
 
 
 def solution(mesh):

time: 72.5 us -> 174 us (2.40)
  Pallas kernels: 64.1 us -> 172 us
  local copies, waits for them, and re-layouts: 6.35 us -> 0 us
    pallas_call x1 -> x2, Pallas kernels: 64.1 us -> 172 us  [the longest x1 104 us: on_device(): pl.pallas_call(finish, out_shape=shapes, in_specs=[anywhere] * 6, out_spe...]
    unnamed x16 -> x0, local copies, waits for them, and re-layouts: 6.35 us -> none
where the time goes in v3:
time: 174 us
  Pallas kernels  172 us (99%)
  between operations  1.93 us (1%)
    pallas_call x1, Pallas kernels, on_device(): pl.pallas_call(finish, out_shape=shapes, in_specs=[anywhere] * 6, out_spe...  104 us
    pallas_call x1, Pallas kernels, on_device(): pl.pallas_call(lambda *refs: kernel(n_grp, heads_per, *refs), out_shape=s...  67.3 us

profile of v3, /device:TPU:1, one launch (start us, length us, event | category | flops | bytes accessed | tf_op | source)
XLA Modules:
  0.0 173.8 jit_solution(3629150920561778118)
XLA Ops:
  1.9 67.3 %grpo_attention.1 = (bf16[1,1,256,2560]{3,2,1,0:T(8,128)(2,1)}, bf16[1,1,256,2560]{3,2,1,0:T(8,128)(2,1)}, bf16[1,1,256,512]{3,2,1,0:T(8,128)(2,1)}, bf16[1,1,25...) custom-call(bf16[1,1,256,2560]{3,2,1,0:T(8,128)(2,1)} %refs_0_.1, ...), custom_call_target="tpu_custom_call" | custom-call | tf_op jit(solution)/shard_map/grpo_attention/pallas_call | solution.py:563
  69.3 104.5 %write_results.1 = (bf16[1,1,256,2560]{3,2,1,0:T(8,128)(2,1)}, bf16[1,1,256,2560]{3,2,1,0:T(8,128)(2,1)}, bf16[1,1,256,512]{3,2,1,0:T(8,128)(2,1)}, bf16[1,1,256...) custom-call(bf16[1,1,256,2560]{3,2,1,0:T(8,128)(2,1)} %get-tuple-element.12.refs_0_, ...), custom_call_target="tpu_custom_call" | custom-call | tf_op jit(solution)/shard_map/write_results/pallas_call | solution.py:574

commit v4 on v3

--- a/solution.py
+++ b/solution.py
@@ -25,9 +25,9 @@
 
 
 def kernel(
-    n_grp, heads_per, q_hbm, rk_hbm, rv_hbm, pk_hbm, pv_hbm, og_hbm, len_hbm, rew_hbm,
+    n_grp, heads_per, q_hbm, rk_hbm, rv_hbm, pk_hbm, pv_hbm, og_hbm, len_ref, rew_ref,
     att_hbm, dq_hbm, drk_hbm, drv_hbm, dpk_hbm, dpv_hbm,
-    len_ref, rew_ref, qn, gn, rkn, rvn, kvn, qT, q2, gT, e_st, m_st, m_cur, l_cur, acc, dqa, aux,
+    qn, gn, rkn, rvn, kvn, qT, q2, gT, e_st, m_st, m_cur, l_cur, acc, dqa, aux,
     stat_out, stat_in, snd, rcv, own_part, att_n, dq_n, rg_n, pg_n,
     sem_l, sem_ps, sem_pr, sem_as, sem_ar, sem_bs, sem_br, sem_ss, sem_sr,
     sem_ms, sem_mr, sem_ol, sem_os, sem_or,
@@ -68,8 +68,6 @@
         pltpu.make_async_copy(rk_hbm.at[0, 0, :, ck], rkn.at[0], sem_l.at[3]),
         pltpu.make_async_copy(rv_hbm.at[0, 0, :, ck], rvn.at[0], sem_l.at[4]),
         pltpu.make_async_copy(og_hbm.at[0, 0, :, cq], gn.at[0], sem_l.at[5]),
-        pltpu.make_async_copy(len_hbm, len_ref, sem_l.at[6]),
-        pltpu.make_async_copy(rew_hbm, rew_ref, sem_l.at[7]),
     ]
     for cp in local:
         cp.start()
@@ -167,11 +165,6 @@
             n_blocks, True,
         )
 
-    n_blocks = 8
-    for i in (2, 3, 4):
-        local[i].wait()
-    own_block(0)
-
     pl.semaphore_wait(barrier, len(friends))
 
     pair = [
@@ -182,7 +175,7 @@
         to(rv_hbm.at[0, 0, :, ok], rvn.at[1], sem_ps.at[4], sem_pr.at[4], twin),
         to(og_hbm.at[0, 0, :, oq], gn.at[1], sem_ps.at[5], sem_pr.at[5], twin),
     ]
-    for cp in pair:
+    for cp in pair[:2]:
         cp.start()
 
     twin_rows = pl.ds(pl.multiple_of((1 - c) * piece, piece), piece)
@@ -191,12 +184,13 @@
         for dst, target in ((YM, up), (YP, down), (ZZ, z_to)):
             ag[dst, kv] = [
                 to(
-                    kvn.at[OWN, kv, part, :], kvn.at[dst, kv, part, :],
-                    s_sem.at[dst, kv], r_sem.at[dst, kv], target,
-                )
-                for part, s_sem, r_sem in (
-                    (my_rows, sem_as, sem_ar), (twin_rows, sem_bs, sem_br),
-                )
+                    (pk_hbm, pv_hbm)[kv].at[0, :, ck], kvn.at[dst, kv, my_rows, :],
+                    sem_as.at[dst, kv], sem_ar.at[dst, kv], target,
+                ),
+                to(
+                    kvn.at[OWN, kv, twin_rows, :], kvn.at[dst, kv, twin_rows, :],
+                    sem_bs.at[dst, kv], sem_br.at[dst, kv], target,
+                ),
             ]
     ag_plan = (
         (YM, YY, 0, up), (YM, ZYM, 0, z_to), (YM, ZYM, 1, z_to),
@@ -208,14 +202,16 @@
             to(kvn.at[src, kv], kvn.at[dst, kv], sem_as.at[dst, kv], sem_ar.at[dst, kv], target)
         ]
 
-    for half in (0, 1):
-        for kv in (0, 1):
-            if half == 0:
-                local[kv].wait()
-            else:
-                pair[kv].wait_recv()
-            for dst in (YM, YP, ZZ):
-                ag[dst, kv][half].start()
+    for kv in (0, 1):
+        for dst in (YM, YP, ZZ):
+            ag[dst, kv][0].start()
+    for cp in pair[2:]:
+        cp.start()
+    for kv in (0, 1):
+        local[kv].wait()
+        pair[kv].wait_recv()
+        for dst in (YM, YP, ZZ):
+            ag[dst, kv][1].start()
 
 
     hops = [((twin,), False), ((z_to,), False), ((up, down), False), ((up,), True)]
@@ -247,14 +243,18 @@
             total = total + stat_in[n, slot]
         stat_out[n + 1] = total
 
-    local[6].wait()
-    local[7].wait()
     row_id = lax.broadcasted_iota(jnp.int32, (8, 128), 0)
-    reward_own = rew_ref[0, 0]
+    length_own = jnp.broadcast_to(len_ref[...], (8, 128))
+    reward_own = jnp.broadcast_to(rew_ref[...], (8, 128))
     stat_out[0] = jnp.where(
-        row_id == 0, len_ref[0, 0], jnp.where(row_id == 1, reward_own, reward_own * reward_own)
+        row_id == 0, length_own, jnp.where(row_id == 1, reward_own, reward_own * reward_own)
     )
     hop_start(0)
+
+    n_blocks = 8
+    for i in (2, 3, 4):
+        local[i].wait()
+    own_block(0)
 
     for i in (2, 3, 4):
         pair[i].wait_recv()
@@ -506,21 +506,24 @@
 
 
 def finish(*refs):
-    ins, outs, sems = refs[:6], refs[6:12], refs[12]
-    copies = []
-    for src, dst in zip(ins, outs):
+    ins, outs, bufs, (sem_in, sem_out) = refs[:6], refs[6:12], refs[12:18], refs[18:]
+    loads, stores = [], []
+    for src, dst, buf in zip(ins, outs, bufs):
         total = src.shape[-2]
-        pieces = 4 if src.shape[-1] > 1024 else 2
+        pieces = 4 if src.shape[-1] > 1024 else 1
         step = total // pieces
         lead = (0,) * (len(src.shape) - 2)
         for i in range(pieces):
             part = lead + (pl.ds(i * step, step),)
-            copies.append(
-                pltpu.make_async_copy(src.at[part], dst.at[part], sems.at[len(copies)])
-            )
-            copies[-1].start()
-    for cp in copies:
-        cp.wait()
+            n = len(loads)
+            loads.append(pltpu.make_async_copy(src.at[part], buf.at[part], sem_in.at[n]))
+            stores.append(pltpu.make_async_copy(buf.at[part], dst.at[part], sem_out.at[n]))
+            loads[-1].start()
+    for load, store in zip(loads, stores):
+        load.wait()
+        store.start()
+    for store in stores:
+        store.wait()
 
 
 def on_device(n_grp, queries, resp_keys, resp_values, prompt_keys, prompt_values, out_grad,
@@ -536,7 +539,6 @@
     dma = pltpu.SemaphoreType.DMA
     vmem = pltpu.VMEM
     scratch = [
-        pltpu.SMEM((1, 1), jnp.int32), pltpu.SMEM((1, 1), jnp.int32),
         vmem((2, rows, half_q), BF16), vmem((2, rows, half_q), BF16),
         vmem((2, rows, half_k), BF16), vmem((2, rows, half_k), BF16),
         vmem((8, 2, blk, half_k), BF16),
@@ -550,7 +552,7 @@
         vmem((2, half_k, blk), F32),
         vmem((2, rows, half_q), BF16), vmem((2, rows, half_q), BF16),
         vmem((2, 2, rows, half_k), BF16), vmem((2, blk, half_k), BF16),
-        dma((8,)), dma((6,)), dma((6,)), dma((8, 2)), dma((8, 2)),
+        dma((6,)), dma((6,)), dma((6,)), dma((8, 2)), dma((8, 2)),
         dma((8, 2)), dma((8, 2)),
         dma((8, 2)), dma((8, 2)),
         dma((7, 2)), dma((7, 2)), dma((6,)), dma((6,)), dma((6,)),
@@ -563,7 +565,7 @@
     results = pl.pallas_call(
         lambda *refs: kernel(n_grp, heads_per, *refs),
         out_shape=shapes,
-        in_specs=[anywhere] * 6 + [pl.BlockSpec(memory_space=pltpu.HBM)] * 2,
+        in_specs=[anywhere] * 6 + [pl.BlockSpec(memory_space=pltpu.VMEM)] * 2,
         out_specs=(anywhere,) * 6,
         scratch_shapes=scratch,
         compiler_params=pltpu.CompilerParams(
@@ -576,7 +578,7 @@
         out_shape=shapes,
         in_specs=[anywhere] * 6,
         out_specs=(anywhere,) * 6,
-        scratch_shapes=[dma((16,))],
+        scratch_shapes=[vmem(x.shape, x.dtype) for x in shapes] + [dma((12,)), dma((12,))],
         compiler_params=pltpu.CompilerParams(vmem_limit_bytes=60 * 2**20),
         name="write_results",
     )(*results)

time: 174 us -> 72.2 us (0.41)
  Pallas kernels: 172 us -> 70.1 us
    pallas_call x1, Pallas kernels: 104 us -> 2.92 us  [on_device(): pl.pallas_call(finish, out_shape=shapes, in_specs=[anywhere] * 6, out_spe...]
where the time goes in v4:
time: 72.2 us; the launch traced here: 72 us
  Pallas kernels  70.1 us (97%)
  between operations  1.93 us (3%)
    pallas_call x1, Pallas kernels, on_device(): pl.pallas_call(lambda *refs: kernel(n_grp, heads_per, *refs), out_shape=s...  67.2 us
    pallas_call x1, Pallas kernels, on_device(): pl.pallas_call(finish, out_shape=shapes, in_specs=[anywhere] * 6, out_spe...  2.92 us

profile of v4, /device:TPU:1, one launch (start us, length us, event | category | flops | bytes accessed | tf_op | source)
XLA Modules:
  0.0 72.0 jit_solution(5285797421118305225)
XLA Ops:
  1.9 67.2 %grpo_attention.1 = (bf16[1,1,256,2560]{3,2,1,0:T(8,128)(2,1)}, bf16[1,1,256,2560]{3,2,1,0:T(8,128)(2,1)}, bf16[1,1,256,512]{3,2,1,0:T(8,128)(2,1)}, bf16[1,1,25...) custom-call(bf16[1,1,256,2560]{3,2,1,0:T(8,128)(2,1)} %refs_0_.1, ...), custom_call_target="tpu_custom_call" | custom-call | tf_op jit(solution)/shard_map/grpo_attention/pallas_call | solution.py:565
  69.1 2.9 %write_results.1 = (bf16[1,1,256,2560]{3,2,1,0:T(8,128)(2,1)}, bf16[1,1,256,2560]{3,2,1,0:T(8,128)(2,1)}, bf16[1,1,256,512]{3,2,1,0:T(8,128)(2,1)}, bf16[1,1,256...) custom-call(bf16[1,1,256,2560]{3,2,1,0:T(8,128)(2,1)} %get-tuple-element.12.refs_0_, ...), custom_call_target="tpu_custom_call" | custom-call | tf_op jit(solution)/shard_map/write_results/pallas_call | solution.py:576

commit v5 on v4

--- a/solution.py
+++ b/solution.py
@@ -27,7 +27,7 @@
 def kernel(
     n_grp, heads_per, q_hbm, rk_hbm, rv_hbm, pk_hbm, pv_hbm, og_hbm, len_ref, rew_ref,
     att_hbm, dq_hbm, drk_hbm, drv_hbm, dpk_hbm, dpv_hbm,
-    qn, gn, rkn, rvn, kvn, qT, q2, gT, e_st, m_st, m_cur, l_cur, acc, dqa, aux,
+    qn, gn, rkn, rvn, kn, vn, stat_own, qT, q2, gT, e_st, m_st, m_cur, l_cur, acc, dqa, aux,
     stat_out, stat_in, snd, rcv, own_part, att_n, dq_n, rg_n, pg_n,
     sem_l, sem_ps, sem_pr, sem_as, sem_ar, sem_bs, sem_br, sem_ss, sem_sr,
     sem_ms, sem_mr, sem_ol, sem_os, sem_or,
@@ -60,10 +60,17 @@
     ck = pl.ds(pl.multiple_of(c * half_k, half_k), half_k)
     ok = pl.ds(pl.multiple_of((1 - c) * half_k, half_k), half_k)
     my_rows = pl.ds(pl.multiple_of(c * piece, piece), piece)
+    tall = piece + 16
+    my_keys = pl.ds(pl.multiple_of(c * tall, 16), piece)
+    my_stats = pl.ds(pl.multiple_of(c * tall + piece, 16), 16)
+    my_part, twin_part = [
+        [pl.ds(pl.multiple_of(k * size, 16), size) for size in (tall, piece)] for k in (c, 1 - c)
+    ]
+    ring_kv = (kn, vn)
 
     local = [
-        pltpu.make_async_copy(pk_hbm.at[0, :, ck], kvn.at[OWN, 0, my_rows, :], sem_l.at[0]),
-        pltpu.make_async_copy(pv_hbm.at[0, :, ck], kvn.at[OWN, 1, my_rows, :], sem_l.at[1]),
+        pltpu.make_async_copy(pk_hbm.at[0, :, ck], kn.at[OWN, my_keys, :], sem_l.at[0]),
+        pltpu.make_async_copy(pv_hbm.at[0, :, ck], vn.at[OWN, my_rows, :], sem_l.at[1]),
         pltpu.make_async_copy(q_hbm.at[0, 0, :, cq], qn.at[0], sem_l.at[2]),
         pltpu.make_async_copy(rk_hbm.at[0, 0, :, ck], rkn.at[0], sem_l.at[3]),
         pltpu.make_async_copy(rv_hbm.at[0, 0, :, ck], rvn.at[0], sem_l.at[4]),
@@ -165,32 +172,38 @@
             n_blocks, True,
         )
 
+    row_id = lax.broadcasted_iota(jnp.int32, stat_own.shape, 0)
+    stat_own[...] = jnp.where(
+        row_id == 0,
+        jnp.broadcast_to(len_ref[...], stat_own.shape),
+        jnp.broadcast_to(rew_ref[...], stat_own.shape),
+    ).astype(F32).astype(BF16)
+    kn[OWN, my_stats, :] = stat_own[...]
     pl.semaphore_wait(barrier, len(friends))
 
     pair = [
-        to(pk_hbm.at[0, :, ok], kvn.at[OWN, 0, my_rows, :], sem_ps.at[0], sem_pr.at[0], twin),
-        to(pv_hbm.at[0, :, ok], kvn.at[OWN, 1, my_rows, :], sem_ps.at[1], sem_pr.at[1], twin),
+        to(pk_hbm.at[0, :, ok], kn.at[OWN, my_keys, :], sem_ps.at[0], sem_pr.at[0], twin),
+        to(pv_hbm.at[0, :, ok], vn.at[OWN, my_rows, :], sem_ps.at[1], sem_pr.at[1], twin),
         to(q_hbm.at[0, 0, :, oq], qn.at[1], sem_ps.at[2], sem_pr.at[2], twin),
         to(rk_hbm.at[0, 0, :, ok], rkn.at[1], sem_ps.at[3], sem_pr.at[3], twin),
         to(rv_hbm.at[0, 0, :, ok], rvn.at[1], sem_ps.at[4], sem_pr.at[4], twin),
         to(og_hbm.at[0, 0, :, oq], gn.at[1], sem_ps.at[5], sem_pr.at[5], twin),
+        to(stat_own, kn.at[OWN, my_stats, :], sem_ps.at[6], sem_pr.at[6], twin),
     ]
-    for cp in pair[:2]:
+    for cp in (pair[0], pair[6], pair[1]):
         cp.start()
 
-    twin_rows = pl.ds(pl.multiple_of((1 - c) * piece, piece), piece)
     ag = {}
     for kv in (0, 1):
         for dst, target in ((YM, up), (YP, down), (ZZ, z_to)):
             ag[dst, kv] = [
                 to(
-                    (pk_hbm, pv_hbm)[kv].at[0, :, ck], kvn.at[dst, kv, my_rows, :],
-                    sem_as.at[dst, kv], sem_ar.at[dst, kv], target,
-                ),
-                to(
-                    kvn.at[OWN, kv, twin_rows, :], kvn.at[dst, kv, twin_rows, :],
-                    sem_bs.at[dst, kv], sem_br.at[dst, kv], target,
-                ),
+                    ring_kv[kv].at[OWN, part[kv], :], ring_kv[kv].at[dst, part[kv], :],
+                    s_sem.at[dst, kv], r_sem.at[dst, kv], target,
+                )
+                for part, s_sem, r_sem in (
+                    (my_part, sem_as, sem_ar), (twin_part, sem_bs, sem_br),
+                )
             ]
     ag_plan = (
         (YM, YY, 0, up), (YM, ZYM, 0, z_to), (YM, ZYM, 1, z_to),
@@ -199,22 +212,24 @@
     )
     for src, dst, kv, target in ag_plan:
         ag[dst, kv] = [
-            to(kvn.at[src, kv], kvn.at[dst, kv], sem_as.at[dst, kv], sem_ar.at[dst, kv], target)
+            to(ring_kv[kv].at[src], ring_kv[kv].at[dst], sem_as.at[dst, kv], sem_ar.at[dst, kv], target)
         ]
 
     for kv in (0, 1):
+        local[kv].wait()
         for dst in (YM, YP, ZZ):
             ag[dst, kv][0].start()
-    for cp in pair[2:]:
+    for cp in pair[2:6]:
         cp.start()
     for kv in (0, 1):
-        local[kv].wait()
         pair[kv].wait_recv()
+        if kv == 0:
+            pair[6].wait_recv()
         for dst in (YM, YP, ZZ):
             ag[dst, kv][1].start()
 
 
-    hops = [((twin,), False), ((z_to,), False), ((up, down), False), ((up,), True)]
+    hops = []
     if ring == 4:
         hops += [((x_up, x_down), False), ((x_up,), True)]
     if n_grp > ring:
@@ -243,14 +258,6 @@
             total = total + stat_in[n, slot]
         stat_out[n + 1] = total
 
-    row_id = lax.broadcasted_iota(jnp.int32, (8, 128), 0)
-    length_own = jnp.broadcast_to(len_ref[...], (8, 128))
-    reward_own = jnp.broadcast_to(rew_ref[...], (8, 128))
-    stat_out[0] = jnp.where(
-        row_id == 0, length_own, jnp.where(row_id == 1, reward_own, reward_own * reward_own)
-    )
-    hop_start(0)
-
     n_blocks = 8
     for i in (2, 3, 4):
         local[i].wait()
@@ -263,8 +270,11 @@
     pair[5].wait_recv()
     for r in range(2):
         turn(gn, gT, r)
-    hop_end(0)
-    hop_start(1)
+    def keys_of(block, j):
+        heads = slice(j * DH, (j + 1) * DH)
+        return jnp.concatenate(
+            [kn[block, 0:piece, heads], kn[block, tall:tall + piece, heads]], axis=0
+        )
 
     def pass_on(waits, starts):
         for key in waits:
@@ -304,36 +314,33 @@
         def _():
             pass_on([(ZYY, 0), (ZYY, 1)], [])
 
-        for n in range(1, len(hops)):
-            @pl.when(step == n)
-            def _():
-                hop_end(n)
-                if n + 1 < len(hops):
-                    hop_start(n + 1)
-
         order = (0, 2, 1, 3)
         forward(
             order,
-            {u: kvn[step, 0, :, (u % 2) * DH:(u % 2 + 1) * DH] for u in order},
-            {u: kvn[step, 1, :, (u % 2) * DH:(u % 2 + 1) * DH] for u in order},
+            {u: keys_of(step, u % 2) for u in order},
+            {u: vn[step, :, (u % 2) * DH:(u % 2 + 1) * DH] for u in order},
             step, False,
         )
 
-    resp_hops = 4
-    sum_one = stat_out[resp_hops, 1:2, :]
-    sum_two = stat_out[resp_hops, 2:3, :]
-    live = stat_out[len(hops), 0:1, :]
+    sum_one = sum_two = live = jnp.zeros((1, 128), F32)
+    for slot in range(n_blocks):
+        for core in range(2):
+            stat = kn[slot, core * tall + piece:(core + 1) * tall, 0:128].astype(F32)
+            live = live + stat[0:1]
+            sum_one = sum_one + stat[1:2]
+            sum_two = sum_two + stat[1:2] * stat[1:2]
+    stat_out[0] = jnp.broadcast_to(live, (8, 128))
+    if hops:
+        hop_start(0)
     n_resp = 16
-    sum_one = sum_one.astype(F32)
-    sum_two = sum_two.astype(F32)
     mean = sum_one / n_resp
     variance = (n_resp * sum_two - sum_one * sum_one) / (n_resp * n_resp)
     spread = jnp.maximum(jnp.sqrt(variance), 1.0)
-    norm = (n_grp * n_resp * rows) / live.astype(F32)
+    twin_stats = pl.ds(pl.multiple_of((1 - c) * tall + piece, 16), 16)
     for r in range(2):
-        length = stat_out[0, 0:1, :] if r == 0 else stat_in[0, 0, 0:1, :]
-        reward = stat_out[0, 1:2, :] if r == 0 else stat_in[0, 0, 1:2, :]
-        strength = (reward.astype(F32) - mean) / spread * norm
+        stat = stat_own[:, 0:128] if r == 0 else kn[OWN, twin_stats, 0:128]
+        length = stat.astype(F32)[0:1].astype(jnp.int32)
+        strength = (stat.astype(F32)[1:2] - mean) / spread
         weight = jnp.concatenate(
             [
                 jnp.where(
@@ -414,12 +421,19 @@
 
     @pl.loop(0, n_blocks)
     def backward_step(step):
+        for n in range(len(hops)):
+            @pl.when(step == 2 * (n + 1))
+            def _():
+                hop_end(n)
+                if n + 1 < len(hops):
+                    hop_start(n + 1)
+
         block = n_blocks - 1 - step
         order = (0, 2, 1, 3)
         sums = backward(
             order,
-            {u: kvn[block, 0, :, (u % 2) * DH:(u % 2 + 1) * DH] for u in order},
-            {u: kvn[block, 1, :, (u % 2) * DH:(u % 2 + 1) * DH] for u in order},
+            {u: keys_of(block, u % 2) for u in order},
+            {u: vn[block, :, (u % 2) * DH:(u % 2 + 1) * DH] for u in order},
             block, lambda u: u % 2,
         )
         total_heads = 4 * heads_per
@@ -449,6 +463,9 @@
     att_twin = to(att_n.at[1], att_hbm.at[0, 0, :, cq], sem_os.at[0], sem_or.at[0], twin)
     att_own.start()
     att_twin.start()
+
+    norm = (n_grp * n_resp * rows) / stat_out[len(hops), 0:1, :]
+    norm_rows = jnp.concatenate([norm] * (rows // 128), axis=1)
 
     outs_own = [
         pltpu.make_async_copy(rg_n.at[0, 0], drk_hbm.at[0, 0, :, ck], sem_ol.at[1]),
@@ -471,19 +488,20 @@
         for j in range(2):
             for h in range(heads_per):
                 col = slice((j * heads_per + h) * DH, (j * heads_per + h + 1) * DH)
-                grad = dqa[2 * r + j, :, h * rows:(h + 1) * rows] * inv_root
+                grad = dqa[2 * r + j, :, h * rows:(h + 1) * rows] * (norm_rows * inv_root)
                 dq_n[r, :, col] = grad.astype(BF16).T
         for (u, kv), term in sums.items():
-            rg_n[r, kv, :, (u % 2) * DH:(u % 2 + 1) * DH] = term.astype(BF16).T
+            rg_n[r, kv, :, (u % 2) * DH:(u % 2 + 1) * DH] = (term * norm_rows).astype(BF16).T
         for cp in outs_twin if r else outs_own:
             cp.start()
 
+    twin_rows = pl.ds(pl.multiple_of((1 - c) * piece, piece), piece)
     for kv, out in enumerate((dpk_hbm, dpv_hbm)):
         total = own_part[kv]
         for name in ("m5", "m7", "m4"):
             msg[name, kv].wait_recv()
             total = total + rcv[names.index(name), kv].astype(F32)
-        pg_n[kv] = total.astype(BF16).T
+        pg_n[kv] = (total * norm_rows).astype(BF16).T
         outs_own.append(
             pltpu.make_async_copy(pg_n.at[kv, my_rows, :], out.at[0, :, ck], sem_ol.at[4 + kv])
         )
@@ -541,18 +559,19 @@
     scratch = [
         vmem((2, rows, half_q), BF16), vmem((2, rows, half_q), BF16),
         vmem((2, rows, half_k), BF16), vmem((2, rows, half_k), BF16),
-        vmem((8, 2, blk, half_k), BF16),
+        vmem((8, blk + 32, half_k), BF16), vmem((8, blk, half_k), BF16),
+        vmem((16, half_k), BF16),
         vmem((4, DH, width), BF16), vmem((4, 2 * DH, width), BF16), vmem((4, DH, width), BF16),
         vmem((9, 4, blk, width), BF16),
         vmem((9, 8, width), F32), vmem((8, width), F32), vmem((8, width), F32),
         vmem((4, DH, width), F32), vmem((4, DH, width), F32),
         vmem((2, 8, width), F32),
-        vmem((8, 8, 128), jnp.int32), vmem((8, 2, 8, 128), jnp.int32),
+        vmem((8, 8, 128), F32), vmem((8, 2, 8, 128), F32),
         vmem((7, 2, half_k, blk), BF16), vmem((7, 2, half_k, blk), BF16),
         vmem((2, half_k, blk), F32),
         vmem((2, rows, half_q), BF16), vmem((2, rows, half_q), BF16),
         vmem((2, 2, rows, half_k), BF16), vmem((2, blk, half_k), BF16),
-        dma((6,)), dma((6,)), dma((6,)), dma((8, 2)), dma((8, 2)),
+        dma((6,)), dma((7,)), dma((7,)), dma((8, 2)), dma((8, 2)),
         dma((8, 2)), dma((8, 2)),
         dma((8, 2)), dma((8, 2)),
         dma((7, 2)), dma((7, 2)), dma((6,)), dma((6,)), dma((6,)),

time: 72.2 us -> 66.4 us (0.920)
  Pallas kernels: 70.1 us -> 64.3 us
    pallas_call x1, Pallas kernels: 67.2 us -> 61.4 us  [on_device(): pl.pallas_call(lambda *refs: kernel(n_grp, heads_per, *refs), out_shape=s...]
where the time goes in v5:
time: 66.4 us; the launch traced here: 66.2 us
  Pallas kernels  64.3 us (97%)
  between operations  1.93 us (3%)
    pallas_call x1, Pallas kernels, on_device(): pl.pallas_call(lambda *refs: kernel(n_grp, heads_per, *refs), out_shape=s...  61.4 us
    pallas_call x1, Pallas kernels, on_device(): pl.pallas_call(finish, out_shape=shapes, in_specs=[anywhere] * 6, out_spe...  2.92 us

profile of v5, /device:TPU:1, one launch (start us, length us, event | category | flops | bytes accessed | tf_op | source)
XLA Modules:
  0.0 66.2 jit_solution(16977789502545719390)
XLA Ops:
  1.9 61.4 %grpo_attention.1 = (bf16[1,1,256,2560]{3,2,1,0:T(8,128)(2,1)}, bf16[1,1,256,2560]{3,2,1,0:T(8,128)(2,1)}, bf16[1,1,256,512]{3,2,1,0:T(8,128)(2,1)}, bf16[1,1,25...) custom-call(bf16[1,1,256,2560]{3,2,1,0:T(8,128)(2,1)} %refs_0_.1, ...), custom_call_target="tpu_custom_call" | custom-call | tf_op jit(solution)/shard_map/grpo_attention/pallas_call | solution.py:584
  63.3 2.9 %write_results.1 = (bf16[1,1,256,2560]{3,2,1,0:T(8,128)(2,1)}, bf16[1,1,256,2560]{3,2,1,0:T(8,128)(2,1)}, bf16[1,1,256,512]{3,2,1,0:T(8,128)(2,1)}, bf16[1,1,256...) custom-call(bf16[1,1,256,2560]{3,2,1,0:T(8,128)(2,1)} %get-tuple-element.12.refs_0_, ...), custom_call_target="tpu_custom_call" | custom-call | tf_op jit(solution)/shard_map/write_results/pallas_call | solution.py:595

commit v6 on v5

--- a/solution.py
+++ b/solution.py
@@ -234,6 +234,16 @@
         hops += [((x_up, x_down), False), ((x_up,), True)]
     if n_grp > ring:
         hops.append(((across,), False))
+    n_cross = len(hops)
+    hops += [((twin,), False), ((z_to,), False), ((up, down), False), ((up,), True)]
+    hop_marks = (-2, -1, 3, 4, 5, 6, 8)[3 - n_cross:]
+
+    def hop_at(mark):
+        for n, own_mark in enumerate(hop_marks):
+            if own_mark == mark:
+                hop_end(n)
+                if n + 1 < len(hops):
+                    hop_start(n + 1)
 
     def hop_copies(n):
         targets, relay = hops[n]
@@ -258,6 +268,9 @@
             total = total + stat_in[n, slot]
         stat_out[n + 1] = total
 
+    stat_out[0] = jnp.broadcast_to(len_ref[...], (8, 128)).astype(F32)
+    hop_start(0)
+
     n_blocks = 8
     for i in (2, 3, 4):
         local[i].wait()
@@ -270,6 +283,7 @@
     pair[5].wait_recv()
     for r in range(2):
         turn(gn, gT, r)
+    hop_at(-2)
     def keys_of(block, j):
         heads = slice(j * DH, (j + 1) * DH)
         return jnp.concatenate(
@@ -322,16 +336,13 @@
             step, False,
         )
 
-    sum_one = sum_two = live = jnp.zeros((1, 128), F32)
+    hop_at(-1)
+    sum_one = sum_two = jnp.zeros((1, 128), F32)
     for slot in range(n_blocks):
         for core in range(2):
             stat = kn[slot, core * tall + piece:(core + 1) * tall, 0:128].astype(F32)
-            live = live + stat[0:1]
             sum_one = sum_one + stat[1:2]
             sum_two = sum_two + stat[1:2] * stat[1:2]
-    stat_out[0] = jnp.broadcast_to(live, (8, 128))
-    if hops:
-        hop_start(0)
     n_resp = 16
     mean = sum_one / n_resp
     variance = (n_resp * sum_two - sum_one * sum_one) / (n_resp * n_resp)
@@ -421,12 +432,11 @@
 
     @pl.loop(0, n_blocks)
     def backward_step(step):
-        for n in range(len(hops)):
-            @pl.when(step == 2 * (n + 1))
-            def _():
-                hop_end(n)
-                if n + 1 < len(hops):
-                    hop_start(n + 1)
+        for mark in hop_marks:
+            if 0 <= mark < n_blocks:
+                @pl.when(step == mark)
+                def _():
+                    hop_at(mark)
 
         block = n_blocks - 1 - step
         order = (0, 2, 1, 3)
@@ -463,9 +473,6 @@
     att_twin = to(att_n.at[1], att_hbm.at[0, 0, :, cq], sem_os.at[0], sem_or.at[0], twin)
     att_own.start()
     att_twin.start()
-
-    norm = (n_grp * n_resp * rows) / stat_out[len(hops), 0:1, :]
-    norm_rows = jnp.concatenate([norm] * (rows // 128), axis=1)
 
     outs_own = [
         pltpu.make_async_copy(rg_n.at[0, 0], drk_hbm.at[0, 0, :, ck], sem_ol.at[1]),
@@ -485,6 +492,10 @@
             {u: rvn[r, :, (u % 2) * DH:(u % 2 + 1) * DH] for u in units},
             n_blocks, lambda u: u,
         )
+        if r == 1:
+            hop_at(n_blocks)
+            norm = (n_grp * n_resp * rows) / stat_out[len(hops), 0:1, :]
+            norm_rows = jnp.concatenate([norm] * (rows // 128), axis=1)
         for j in range(2):
             for h in range(heads_per):
                 col = slice((j * heads_per + h) * DH, (j * heads_per + h + 1) * DH)

time: 66.4 us -> 67.9 us (1.023)
  Pallas kernels: 64.3 us -> 65.8 us
    pallas_call x1, Pallas kernels: 61.4 us -> 62.9 us  [on_device(): pl.pallas_call(lambda *refs: kernel(n_grp, heads_per, *refs), out_shape=s...]
where the time goes in v6:
time: 67.9 us; the launch traced here: 67.7 us
  Pallas kernels  65.8 us (97%)
  between operations  1.93 us (3%)
    pallas_call x1, Pallas kernels, on_device(): pl.pallas_call(lambda *refs: kernel(n_grp, heads_per, *refs), out_shape=s...  62.9 us
    pallas_call x1, Pallas kernels, on_device(): pl.pallas_call(finish, out_shape=shapes, in_specs=[anywhere] * 6, out_spe...  2.92 us

profile of v6, /device:TPU:1, one launch (start us, length us, event | category | flops | bytes accessed | tf_op | source)
XLA Modules:
  0.0 67.7 jit_solution(47886029245277176)
XLA Ops:
  1.9 62.9 %grpo_attention.1 = (bf16[1,1,256,2560]{3,2,1,0:T(8,128)(2,1)}, bf16[1,1,256,2560]{3,2,1,0:T(8,128)(2,1)}, bf16[1,1,256,512]{3,2,1,0:T(8,128)(2,1)}, bf16[1,1,25...) custom-call(bf16[1,1,256,2560]{3,2,1,0:T(8,128)(2,1)} %refs_0_.1, ...), custom_call_target="tpu_custom_call" | custom-call | tf_op jit(solution)/shard_map/grpo_attention/pallas_call | solution.py:595
  64.8 2.9 %write_results.1 = (bf16[1,1,256,2560]{3,2,1,0:T(8,128)(2,1)}, bf16[1,1,256,2560]{3,2,1,0:T(8,128)(2,1)}, bf16[1,1,256,512]{3,2,1,0:T(8,128)(2,1)}, bf16[1,1,256...) custom-call(bf16[1,1,256,2560]{3,2,1,0:T(8,128)(2,1)} %get-tuple-element.12.refs_0_, ...), custom_call_target="tpu_custom_call" | custom-call | tf_op jit(solution)/shard_map/write_results/pallas_call | solution.py:606

commit v7 on v5

--- a/solution.py
+++ b/solution.py
@@ -81,16 +81,8 @@
 
     twin = at(0, 0, 1)
     z_to, up, down = at(1, 0, 0), at(0, 1, 0), at(0, 3, 0)
-    ring = min(4, n_grp)
-    base = (grp // ring) * ring
-    x_up = {"grp": base + (grp - base + 1) % ring}
-    x_down = {"grp": base + (grp - base + ring - 1) % ring}
-    across = {"grp": (grp + ring) % n_grp}
-    friends = [twin, z_to, up, down]
-    if ring == 4:
-        friends += [x_up, x_down]
-    if n_grp > ring:
-        friends.append(across)
+    groups = [{"grp": (grp + dg) % n_grp} for dg in range(1, n_grp)]
+    friends = [twin, z_to, up, down] + groups
     barrier = pltpu.get_barrier_semaphore()
     for friend in friends:
         pl.semaphore_signal(barrier, inc=1, device_id=friend, device_id_type=MESH)
@@ -229,35 +221,6 @@
             ag[dst, kv][1].start()
 
 
-    hops = []
-    if ring == 4:
-        hops += [((x_up, x_down), False), ((x_up,), True)]
-    if n_grp > ring:
-        hops.append(((across,), False))
-
-    def hop_copies(n):
-        targets, relay = hops[n]
-        src = stat_in.at[n - 1, 1] if relay else stat_out.at[n]
-        copies = []
-        for i, target in enumerate(targets):
-            slot = 1 - i if len(targets) == 2 else 0
-            copies.append(
-                to(src, stat_in.at[n, slot], sem_ss.at[n, slot], sem_sr.at[n, slot], target)
-            )
-        return copies
-
-    def hop_start(n):
-        for cp in hop_copies(n):
-            cp.start()
-
-    def hop_end(n):
-        for cp in hop_copies(n):
-            cp.wait_recv()
-        total = stat_out[n]
-        for slot in range(len(hops[n][0])):
-            total = total + stat_in[n, slot]
-        stat_out[n + 1] = total
-
     n_blocks = 8
     for i in (2, 3, 4):
         local[i].wait()
@@ -329,9 +292,16 @@
             live = live + stat[0:1]
             sum_one = sum_one + stat[1:2]
             sum_two = sum_two + stat[1:2] * stat[1:2]
-    stat_out[0] = jnp.broadcast_to(live, (8, 128))
-    if hops:
-        hop_start(0)
+    stat_out[...] = jnp.broadcast_to(live, (8, 128))
+    counts = [
+        to(
+            stat_out, stat_in.at[n_grp - dg], sem_ss.at[n_grp - dg], sem_sr.at[n_grp - dg],
+            groups[dg - 1],
+        )
+        for dg in range(1, n_grp)
+    ]
+    for cp in counts:
+        cp.start()
     n_resp = 16
     mean = sum_one / n_resp
     variance = (n_resp * sum_two - sum_one * sum_one) / (n_resp * n_resp)
@@ -421,13 +391,6 @@
 
     @pl.loop(0, n_blocks)
     def backward_step(step):
-        for n in range(len(hops)):
-            @pl.when(step == 2 * (n + 1))
-            def _():
-                hop_end(n)
-                if n + 1 < len(hops):
-                    hop_start(n + 1)
-
         block = n_blocks - 1 - step
         order = (0, 2, 1, 3)
         sums = backward(
@@ -464,9 +427,6 @@
     att_own.start()
     att_twin.start()
 
-    norm = (n_grp * n_resp * rows) / stat_out[len(hops), 0:1, :]
-    norm_rows = jnp.concatenate([norm] * (rows // 128), axis=1)
-
     outs_own = [
         pltpu.make_async_copy(rg_n.at[0, 0], drk_hbm.at[0, 0, :, ck], sem_ol.at[1]),
         pltpu.make_async_copy(rg_n.at[0, 1], drv_hbm.at[0, 0, :, ck], sem_ol.at[2]),
@@ -485,6 +445,13 @@
             {u: rvn[r, :, (u % 2) * DH:(u % 2 + 1) * DH] for u in units},
             n_blocks, lambda u: u,
         )
+        if r == 1:
+            for cp in counts:
+                cp.wait_recv()
+            for slot in range(1, n_grp):
+                live = live + stat_in[slot, 0:1, :]
+            norm = (n_grp * n_resp * rows) / live
+            norm_rows = jnp.concatenate([norm] * (rows // 128), axis=1)
         for j in range(2):
             for h in range(heads_per):
                 col = slice((j * heads_per + h) * DH, (j * heads_per + h + 1) * DH)
@@ -518,8 +485,7 @@
         cp.wait()
     for cp in [att_twin] + outs_twin:
         cp.wait()
-    stats = [cp for n in range(len(hops)) for cp in hop_copies(n)]
-    for cp in pair + stats + sum(ag.values(), []) + list(msg.values()):
+    for cp in pair + counts + sum(ag.values(), []) + list(msg.values()):
         cp.wait_send()
 
 
@@ -566,14 +532,13 @@
         vmem((9, 8, width), F32), vmem((8, width), F32), vmem((8, width), F32),
         vmem((4, DH, width), F32), vmem((4, DH, width), F32),
         vmem((2, 8, width), F32),
-        vmem((8, 8, 128), F32), vmem((8, 2, 8, 128), F32),
+        vmem((8, 128), F32), vmem((n_grp, 8, 128), F32),
         vmem((7, 2, half_k, blk), BF16), vmem((7, 2, half_k, blk), BF16),
         vmem((2, half_k, blk), F32),
         vmem((2, rows, half_q), BF16), vmem((2, rows, half_q), BF16),
         vmem((2, 2, rows, half_k), BF16), vmem((2, blk, half_k), BF16),
         dma((6,)), dma((7,)), dma((7,)), dma((8, 2)), dma((8, 2)),
-        dma((8, 2)), dma((8, 2)),
-        dma((8, 2)), dma((8, 2)),
+        dma((8, 2)), dma((8, 2)), dma((n_grp,)), dma((n_grp,)),
         dma((7, 2)), dma((7, 2)), dma((6,)), dma((6,)), dma((6,)),
     ]
     like = lambda a: jax.ShapeDtypeStruct(a.shape, a.dtype)

time: 66.4 us -> 63.8 us (0.961)
  Pallas kernels: 64.3 us -> 61.7 us
    pallas_call x1, Pallas kernels: 61.4 us -> 58.8 us  [on_device(): pl.pallas_call(lambda *refs: kernel(n_grp, heads_per, *refs), out_shape=s...]
where the time goes in v7:
time: 63.8 us; the launch traced here: 63.7 us
  Pallas kernels  61.7 us (97%)
  between operations  1.93 us (3%)
    pallas_call x1, Pallas kernels, on_device(): pl.pallas_call(lambda *refs: kernel(n_grp, heads_per, *refs), out_shape=s...  58.8 us
    pallas_call x1, Pallas kernels, on_device(): pl.pallas_call(finish, out_shape=shapes, in_specs=[anywhere] * 6, out_spe...  2.92 us

profile of v7, /device:TPU:1, one launch (start us, length us, event | category | flops | bytes accessed | tf_op | source)
XLA Modules:
  0.0 63.7 jit_solution(3248588044473762209)
XLA Ops:
  1.9 58.8 %grpo_attention.1 = (bf16[1,1,256,2560]{3,2,1,0:T(8,128)(2,1)}, bf16[1,1,256,2560]{3,2,1,0:T(8,128)(2,1)}, bf16[1,1,256,512]{3,2,1,0:T(8,128)(2,1)}, bf16[1,1,25...) custom-call(bf16[1,1,256,2560]{3,2,1,0:T(8,128)(2,1)} %refs_0_.1, ...), custom_call_target="tpu_custom_call" | custom-call | tf_op jit(solution)/shard_map/grpo_attention/pallas_call | solution.py:549
  60.7 2.9 %write_results.1 = (bf16[1,1,256,2560]{3,2,1,0:T(8,128)(2,1)}, bf16[1,1,256,2560]{3,2,1,0:T(8,128)(2,1)}, bf16[1,1,256,512]{3,2,1,0:T(8,128)(2,1)}, bf16[1,1,256...) custom-call(bf16[1,1,256,2560]{3,2,1,0:T(8,128)(2,1)} %get-tuple-element.12.refs_0_, ...), custom_call_target="tpu_custom_call" | custom-call | tf_op jit(solution)/shard_map/write_results/pallas_call | solution.py:560

commit v8 on v7

--- a/solution.py
+++ b/solution.py
@@ -28,7 +28,7 @@
     n_grp, heads_per, q_hbm, rk_hbm, rv_hbm, pk_hbm, pv_hbm, og_hbm, len_ref, rew_ref,
     att_hbm, dq_hbm, drk_hbm, drv_hbm, dpk_hbm, dpv_hbm,
     qn, gn, rkn, rvn, kn, vn, stat_own, qT, q2, gT, e_st, m_st, m_cur, l_cur, acc, dqa, aux,
-    stat_out, stat_in, snd, rcv, own_part, att_n, dq_n, rg_n, pg_n,
+    stat_out, stat_in, stat_all, snd, rcv, own_part, att_n, dq_n, rg_n, pg_n,
     sem_l, sem_ps, sem_pr, sem_as, sem_ar, sem_bs, sem_br, sem_ss, sem_sr,
     sem_ms, sem_mr, sem_ol, sem_os, sem_or,
 ):
@@ -82,10 +82,15 @@
     twin = at(0, 0, 1)
     z_to, up, down = at(1, 0, 0), at(0, 1, 0), at(0, 3, 0)
     groups = [{"grp": (grp + dg) % n_grp} for dg in range(1, n_grp)]
-    friends = [twin, z_to, up, down] + groups
+    friends = [twin, z_to, up, down]
     barrier = pltpu.get_barrier_semaphore()
     for friend in friends:
         pl.semaphore_signal(barrier, inc=1, device_id=friend, device_id_type=MESH)
+
+    @pl.when(grp == 0)
+    def _():
+        for group in groups:
+            pl.semaphore_signal(barrier, inc=1, device_id=group, device_id_type=MESH)
 
     def turn(src, dst, r):
         for j in range(2):
@@ -171,7 +176,7 @@
         jnp.broadcast_to(rew_ref[...], stat_own.shape),
     ).astype(F32).astype(BF16)
     kn[OWN, my_stats, :] = stat_own[...]
-    pl.semaphore_wait(barrier, len(friends))
+    pl.semaphore_wait(barrier, len(friends) + jnp.minimum(grp, 1))
 
     pair = [
         to(pk_hbm.at[0, :, ok], kn.at[OWN, my_keys, :], sem_ps.at[0], sem_pr.at[0], twin),
@@ -233,6 +238,7 @@
     pair[5].wait_recv()
     for r in range(2):
         turn(gn, gT, r)
+    dqa[...] = jnp.zeros_like(dqa)
     def keys_of(block, j):
         heads = slice(j * DH, (j + 1) * DH)
         return jnp.concatenate(
@@ -293,15 +299,19 @@
             sum_one = sum_one + stat[1:2]
             sum_two = sum_two + stat[1:2] * stat[1:2]
     stat_out[...] = jnp.broadcast_to(live, (8, 128))
-    counts = [
-        to(
-            stat_out, stat_in.at[n_grp - dg], sem_ss.at[n_grp - dg], sem_sr.at[n_grp - dg],
-            groups[dg - 1],
-        )
-        for dg in range(1, n_grp)
-    ]
-    for cp in counts:
-        cp.start()
+
+    def count_in(slot):
+        return to(
+            stat_out, stat_in.at[slot], sem_ss.at[0], sem_sr.at[slot], {"grp": jnp.zeros_like(grp)}
+        )
+
+    def count_back(n):
+        return to(stat_all, stat_all, sem_ss.at[n], sem_sr.at[0], groups[n - 1])
+
+    @pl.when(grp != 0)
+    def _():
+        count_in(grp).start()
+
     n_resp = 16
     mean = sum_one / n_resp
     variance = (n_resp * sum_two - sum_one * sum_one) / (n_resp * n_resp)
@@ -332,7 +342,6 @@
                 )
                 aux[0, u:u + 1, cols] = inv * weight
                 aux[1, u:u + 1, cols] = delta
-                dqa[u, :, cols] = jnp.zeros((DH, rows), F32)
 
     def backward(units, keys, values, block, place):
         flat = {u: k.T for u, k in keys.items()}
@@ -391,6 +400,16 @@
 
     @pl.loop(0, n_blocks)
     def backward_step(step):
+        @pl.when((step == 5) & (grp == 0))
+        def _():
+            total = stat_out[...]
+            for slot in range(1, n_grp):
+                count_in(slot).wait_recv()
+                total = total + stat_in[slot]
+            stat_all[...] = total
+            for n in range(1, n_grp):
+                count_back(n).start()
+
         block = n_blocks - 1 - step
         order = (0, 2, 1, 3)
         sums = backward(
@@ -446,11 +465,11 @@
             n_blocks, lambda u: u,
         )
         if r == 1:
-            for cp in counts:
-                cp.wait_recv()
-            for slot in range(1, n_grp):
-                live = live + stat_in[slot, 0:1, :]
-            norm = (n_grp * n_resp * rows) / live
+            @pl.when(grp != 0)
+            def _():
+                count_back(1).wait_recv()
+
+            norm = (n_grp * n_resp * rows) / stat_all[0:1, :]
             norm_rows = jnp.concatenate([norm] * (rows // 128), axis=1)
         for j in range(2):
             for h in range(heads_per):
@@ -485,7 +504,16 @@
         cp.wait()
     for cp in [att_twin] + outs_twin:
         cp.wait()
-    for cp in pair + counts + sum(ag.values(), []) + list(msg.values()):
+    @pl.when(grp != 0)
+    def _():
+        count_in(grp).wait_send()
+
+    @pl.when(grp == 0)
+    def _():
+        for n in range(1, n_grp):
+            count_back(n).wait_send()
+
+    for cp in pair + sum(ag.values(), []) + list(msg.values()):
         cp.wait_send()
 
 
@@ -532,7 +560,7 @@
         vmem((9, 8, width), F32), vmem((8, width), F32), vmem((8, width), F32),
         vmem((4, DH, width), F32), vmem((4, DH, width), F32),
         vmem((2, 8, width), F32),
-        vmem((8, 128), F32), vmem((n_grp, 8, 128), F32),
+        vmem((8, 128), F32), vmem((n_grp, 8, 128), F32), vmem((8, 128), F32),
         vmem((7, 2, half_k, blk), BF16), vmem((7, 2, half_k, blk), BF16),
         vmem((2, half_k, blk), F32),
         vmem((2, rows, half_q), BF16), vmem((2, rows, half_q), BF16),

time: 63.8 us -> 59.4 us (0.931)
  Pallas kernels: 61.7 us -> 57.3 us
    pallas_call x1, Pallas kernels: 58.8 us -> 54.4 us  [on_device(): pl.pallas_call(lambda *refs: kernel(n_grp, heads_per, *refs), out_shape=s...]
where the time goes in v8:
time: 59.4 us; the launch traced here: 59.2 us
  Pallas kernels  57.3 us (96%)
  between operations  1.93 us (3%)
    pallas_call x1, Pallas kernels, on_device(): pl.pallas_call(lambda *refs: kernel(n_grp, heads_per, *refs), out_shape=s...  54.4 us
    pallas_call x1, Pallas kernels, on_device(): pl.pallas_call(finish, out_shape=shapes, in_specs=[anywhere] * 6, out_spe...  2.92 us

profile of v8, /device:TPU:1, one launch (start us, length us, event | category | flops | bytes accessed | tf_op | source)
XLA Modules:
  0.0 59.2 jit_solution(10403694852055417450)
XLA Ops:
  1.9 54.4 %grpo_attention.1 = (bf16[1,1,256,2560]{3,2,1,0:T(8,128)(2,1)}, bf16[1,1,256,2560]{3,2,1,0:T(8,128)(2,1)}, bf16[1,1,256,512]{3,2,1,0:T(8,128)(2,1)}, bf16[1,1,25...) custom-call(bf16[1,1,256,2560]{3,2,1,0:T(8,128)(2,1)} %refs_0_.1, ...), custom_call_target="tpu_custom_call" | custom-call | tf_op jit(solution)/shard_map/grpo_attention/pallas_call | solution.py:577
  56.3 2.9 %write_results.1 = (bf16[1,1,256,2560]{3,2,1,0:T(8,128)(2,1)}, bf16[1,1,256,2560]{3,2,1,0:T(8,128)(2,1)}, bf16[1,1,256,512]{3,2,1,0:T(8,128)(2,1)}, bf16[1,1,256...) custom-call(bf16[1,1,256,2560]{3,2,1,0:T(8,128)(2,1)} %get-tuple-element.12.refs_0_, ...), custom_call_target="tpu_custom_call" | custom-call | tf_op jit(solution)/shard_map/write_results/pallas_call | solution.py:588

commit v9 on v8

--- a/solution.py
+++ b/solution.py
@@ -63,9 +63,7 @@
     tall = piece + 16
     my_keys = pl.ds(pl.multiple_of(c * tall, 16), piece)
     my_stats = pl.ds(pl.multiple_of(c * tall + piece, 16), 16)
-    my_part, twin_part = [
-        [pl.ds(pl.multiple_of(k * size, 16), size) for size in (tall, piece)] for k in (c, 1 - c)
-    ]
+    twin_part = [pl.ds(pl.multiple_of((1 - c) * size, 16), size) for size in (tall, piece)]
     ring_kv = (kn, vn)
 
     local = [
@@ -195,13 +193,22 @@
         for dst, target in ((YM, up), (YP, down), (ZZ, z_to)):
             ag[dst, kv] = [
                 to(
-                    ring_kv[kv].at[OWN, part[kv], :], ring_kv[kv].at[dst, part[kv], :],
-                    s_sem.at[dst, kv], r_sem.at[dst, kv], target,
+                    (pk_hbm, pv_hbm)[kv].at[0, :, ck],
+                    ring_kv[kv].at[dst, (my_keys, my_rows)[kv], :],
+                    sem_as.at[dst, kv], sem_ar.at[dst, kv], target,
+                ),
+                to(
+                    ring_kv[kv].at[OWN, twin_part[kv], :], ring_kv[kv].at[dst, twin_part[kv], :],
+                    sem_bs.at[dst, kv], sem_br.at[dst, kv], target,
+                ),
+            ]
+            if kv == 0:
+                ag[dst, kv].append(
+                    to(
+                        stat_own, kn.at[dst, my_stats, :], sem_ss.at[n_grp + dst],
+                        sem_sr.at[n_grp + dst], target,
+                    )
                 )
-                for part, s_sem, r_sem in (
-                    (my_part, sem_as, sem_ar), (twin_part, sem_bs, sem_br),
-                )
-            ]
     ag_plan = (
         (YM, YY, 0, up), (YM, ZYM, 0, z_to), (YM, ZYM, 1, z_to),
         (YP, YY, 1, down), (ZZ, ZYP, 0, down), (ZZ, ZYP, 1, down),
@@ -213,12 +220,14 @@
         ]
 
     for kv in (0, 1):
-        local[kv].wait()
         for dst in (YM, YP, ZZ):
             ag[dst, kv][0].start()
     for cp in pair[2:6]:
         cp.start()
+    for dst in (YM, YP, ZZ):
+        ag[dst, 0][2].start()
     for kv in (0, 1):
+        local[kv].wait()
         pair[kv].wait_recv()
         if kv == 0:
             pair[6].wait_recv()
@@ -269,11 +278,11 @@
 
         @pl.when(step == 4)
         def _():
-            pass_on([(ZYM, 1)], [(ZYY, 1)])
+            pass_on([(YY, 0), (YY, 1)], [])
 
         @pl.when(step == 5)
         def _():
-            pass_on([(YY, 0), (YY, 1)], [])
+            pass_on([(ZYM, 1)], [(ZYY, 1)])
 
         @pl.when(step == 6)
         def _():
@@ -283,12 +292,13 @@
         def _():
             pass_on([(ZYY, 0), (ZYY, 1)], [])
 
+        block = step + ((step // 4) % 2) * (1 - (step % 4) // 2) * (1 - 2 * (step % 2))
         order = (0, 2, 1, 3)
         forward(
             order,
-            {u: keys_of(step, u % 2) for u in order},
-            {u: vn[step, :, (u % 2) * DH:(u % 2 + 1) * DH] for u in order},
-            step, False,
+            {u: keys_of(block, u % 2) for u in order},
+            {u: vn[block, :, (u % 2) * DH:(u % 2 + 1) * DH] for u in order},
+            block, False,
         )
 
     sum_one = sum_two = live = jnp.zeros((1, 128), F32)
@@ -377,9 +387,7 @@
             if i >= 1:
                 finish(i - 1)
         finish(len(todo) - 1)
-        return {
-            key: term.T * inv_root if key[1] == 0 else term for key, term in sums.items()
-        }
+        return sums
 
     names = ("m1", "m6", "m3", "m2", "m7", "m5", "m4")
     route = {
@@ -428,7 +436,10 @@
                 u, 0:DH, pl.ds(pl.multiple_of(h * rows, rows), rows)
             ].T
         for (j, kv), term in sums.items():
-            own_part[kv, j * DH:(j + 1) * DH, :] = term
+            if kv == 0:
+                own_part[kv, :, j * DH:(j + 1) * DH] = term
+            else:
+                own_part[kv, j * DH:(j + 1) * DH, :] = term
 
         for n, name in enumerate(names):
             @pl.when(step == n)
@@ -477,7 +488,11 @@
                 grad = dqa[2 * r + j, :, h * rows:(h + 1) * rows] * (norm_rows * inv_root)
                 dq_n[r, :, col] = grad.astype(BF16).T
         for (u, kv), term in sums.items():
-            rg_n[r, kv, :, (u % 2) * DH:(u % 2 + 1) * DH] = (term * norm_rows).astype(BF16).T
+            if kv == 0:
+                done = (term * (norm * inv_root)).astype(BF16)
+            else:
+                done = (term * norm_rows).astype(BF16).T
+            rg_n[r, kv, :, (u % 2) * DH:(u % 2 + 1) * DH] = done
         for cp in outs_twin if r else outs_own:
             cp.start()
 
@@ -487,7 +502,10 @@
         for name in ("m5", "m7", "m4"):
             msg[name, kv].wait_recv()
             total = total + rcv[names.index(name), kv].astype(F32)
-        pg_n[kv] = (total * norm_rows).astype(BF16).T
+        if kv == 0:
+            pg_n[kv] = (total * (norm_rows * inv_root)).astype(BF16)
+        else:
+            pg_n[kv] = (total * norm_rows).astype(BF16).T
         outs_own.append(
             pltpu.make_async_copy(pg_n.at[kv, my_rows, :], out.at[0, :, ck], sem_ol.at[4 + kv])
         )
@@ -566,7 +584,7 @@
         vmem((2, rows, half_q), BF16), vmem((2, rows, half_q), BF16),
         vmem((2, 2, rows, half_k), BF16), vmem((2, blk, half_k), BF16),
         dma((6,)), dma((7,)), dma((7,)), dma((8, 2)), dma((8, 2)),
-        dma((8, 2)), dma((8, 2)), dma((n_grp,)), dma((n_grp,)),
+        dma((8, 2)), dma((8, 2)), dma((n_grp + 8,)), dma((n_grp + 8,)),
         dma((7, 2)), dma((7, 2)), dma((6,)), dma((6,)), dma((6,)),
     ]
     like = lambda a: jax.ShapeDtypeStruct(a.shape, a.dtype)

time: 59.4 us -> 61.1 us (1.029)
  Pallas kernels: 57.3 us -> 59.1 us
    pallas_call x1, Pallas kernels: 54.4 us -> 56.1 us  [on_device(): pl.pallas_call(lambda *refs: kernel(n_grp, heads_per, *refs), out_shape=s...]
where the time goes in v9:
time: 61.1 us; the launch traced here: 61 us
  Pallas kernels  59.1 us (97%)
  between operations  1.93 us (3%)
    pallas_call x1, Pallas kernels, on_device(): pl.pallas_call(lambda *refs: kernel(n_grp, heads_per, *refs), out_shape=s...  56.1 us
    pallas_call x1, Pallas kernels, on_device(): pl.pallas_call(finish, out_shape=shapes, in_specs=[anywhere] * 6, out_spe...  2.92 us

profile of v9, /device:TPU:1, one launch (start us, length us, event | category | flops | bytes accessed | tf_op | source)
XLA Modules:
  0.0 61.0 jit_solution(9391118775715255604)
XLA Ops:
  1.9 56.1 %grpo_attention.1 = (bf16[1,1,256,2560]{3,2,1,0:T(8,128)(2,1)}, bf16[1,1,256,2560]{3,2,1,0:T(8,128)(2,1)}, bf16[1,1,256,512]{3,2,1,0:T(8,128)(2,1)}, bf16[1,1,25...) custom-call(bf16[1,1,256,2560]{3,2,1,0:T(8,128)(2,1)} %refs_0_.1, ...), custom_call_target="tpu_custom_call" | custom-call | tf_op jit(solution)/shard_map/grpo_attention/pallas_call | solution.py:595
  58.1 2.9 %write_results.1 = (bf16[1,1,256,2560]{3,2,1,0:T(8,128)(2,1)}, bf16[1,1,256,2560]{3,2,1,0:T(8,128)(2,1)}, bf16[1,1,256,512]{3,2,1,0:T(8,128)(2,1)}, bf16[1,1,256...) custom-call(bf16[1,1,256,2560]{3,2,1,0:T(8,128)(2,1)} %get-tuple-element.12.refs_0_, ...), custom_call_target="tpu_custom_call" | custom-call | tf_op jit(solution)/shard_map/write_results/pallas_call | solution.py:606

commit v10 on v8

--- a/solution.py
+++ b/solution.py
@@ -377,9 +377,7 @@
             if i >= 1:
                 finish(i - 1)
         finish(len(todo) - 1)
-        return {
-            key: term.T * inv_root if key[1] == 0 else term for key, term in sums.items()
-        }
+        return sums
 
     names = ("m1", "m6", "m3", "m2", "m7", "m5", "m4")
     route = {
@@ -428,7 +426,10 @@
                 u, 0:DH, pl.ds(pl.multiple_of(h * rows, rows), rows)
             ].T
         for (j, kv), term in sums.items():
-            own_part[kv, j * DH:(j + 1) * DH, :] = term
+            if kv == 0:
+                own_part[kv, :, j * DH:(j + 1) * DH] = term
+            else:
+                own_part[kv, j * DH:(j + 1) * DH, :] = term
 
         for n, name in enumerate(names):
             @pl.when(step == n)
@@ -477,7 +478,11 @@
                 grad = dqa[2 * r + j, :, h * rows:(h + 1) * rows] * (norm_rows * inv_root)
                 dq_n[r, :, col] = grad.astype(BF16).T
         for (u, kv), term in sums.items():
-            rg_n[r, kv, :, (u % 2) * DH:(u % 2 + 1) * DH] = (term * norm_rows).astype(BF16).T
+            if kv == 0:
+                done = (term * (norm * inv_root)).astype(BF16)
+            else:
+                done = (term * norm_rows).astype(BF16).T
+            rg_n[r, kv, :, (u % 2) * DH:(u % 2 + 1) * DH] = done
         for cp in outs_twin if r else outs_own:
             cp.start()
 
@@ -487,7 +492,10 @@
         for name in ("m5", "m7", "m4"):
             msg[name, kv].wait_recv()
             total = total + rcv[names.index(name), kv].astype(F32)
-        pg_n[kv] = (total * norm_rows).astype(BF16).T
+        if kv == 0:
+            pg_n[kv] = (total * (norm_rows * inv_root)).astype(BF16)
+        else:
+            pg_n[kv] = (total * norm_rows).astype(BF16).T
         outs_own.append(
             pltpu.make_async_copy(pg_n.at[kv, my_rows, :], out.at[0, :, ck], sem_ol.at[4 + kv])
         )

time: 59.4 us -> 58.9 us (level)
  no operation moved by 1% of the time
where the time goes in v10:
time: 58.9 us; the launch traced here: 58.8 us
  Pallas kernels  56.9 us (97%)
  between operations  1.93 us (3%)
    pallas_call x1, Pallas kernels, on_device(): pl.pallas_call(lambda *refs: kernel(n_grp, heads_per, *refs), out_shape=s...  53.9 us
    pallas_call x1, Pallas kernels, on_device(): pl.pallas_call(finish, out_shape=shapes, in_specs=[anywhere] * 6, out_spe...  2.92 us

profile of v10, /device:TPU:1, one launch (start us, length us, event | category | flops | bytes accessed | tf_op | source)
XLA Modules:
  0.0 58.8 jit_solution(9798745731681900609)
XLA Ops:
  1.9 53.9 %grpo_attention.1 = (bf16[1,1,256,2560]{3,2,1,0:T(8,128)(2,1)}, bf16[1,1,256,2560]{3,2,1,0:T(8,128)(2,1)}, bf16[1,1,256,512]{3,2,1,0:T(8,128)(2,1)}, bf16[1,1,25...) custom-call(bf16[1,1,256,2560]{3,2,1,0:T(8,128)(2,1)} %refs_0_.1, ...), custom_call_target="tpu_custom_call" | custom-call | tf_op jit(solution)/shard_map/grpo_attention/pallas_call | solution.py:585
  55.9 2.9 %write_results.1 = (bf16[1,1,256,2560]{3,2,1,0:T(8,128)(2,1)}, bf16[1,1,256,2560]{3,2,1,0:T(8,128)(2,1)}, bf16[1,1,256,512]{3,2,1,0:T(8,128)(2,1)}, bf16[1,1,256...) custom-call(bf16[1,1,256,2560]{3,2,1,0:T(8,128)(2,1)} %get-tuple-element.12.refs_0_, ...), custom_call_target="tpu_custom_call" | custom-call | tf_op jit(solution)/shard_map/write_results/pallas_call | solution.py:596
